TPU v7x, 128 devices: a whole 4x4x4 slice. The times are simulated.
128 devices in a mesh: clip: 8 (over z, x_hi), seq: 16 (over y, x_lo, core).
Axes of the slice: x: 4 (x_hi: 2, x_lo: 2; x = x_hi * 2 + x_lo), y: 4, z: 4, core: 2. Of those that a mesh axis runs over, the one named last changes fastest.
Arguments:
- x_saved: float32 [8, 16, 256, 1152], P('clip', 'seq'), may hold values from -20 to 20, as said below
- grad_out: float32 [8, 16, 256, 1152], P('clip', 'seq'), may hold values from -6 to 6
- keep_mask: int32 [8, 16, 256], P('clip', 'seq'), may hold values 0 or 1
- w_qkv: float32 [1152, 3456], replicated, may hold values from -0.1620453 to 0.1620453, as said below
- w_out: float32 [1152, 1152], replicated, may hold values from -0.1875 to 0.1875
Outputs:
- grad_input: float32 [8, 16, 256, 1152], P('clip', 'seq')
- grad_w_qkv: float32 [1152, 3456], P('clip', 'seq')
- grad_w_out: float32 [1152, 1152], P('clip', 'seq')
Inputs may be any that keep to these rules, and one draw needn't show every extreme that they name: `x_saved`: saved activations. `w_qkv`: projection entries of order 1152 ** -0.5.
All inputs are finite; a program needn't handle non-finite values. No bound on the sum of `keep_mask` on one device may be relied on, other than what follows from the above.
Results may differ from a plain program's by a relative error of at most 0.0003.
Values sent between devices are 32-bit elements; how exact they have to be, the bound alone decides.
A program may use at most 192 MiB of HBM per device.

v0:
```python
import jax
import jax.numpy as jnp
from jax import lax
from jax.sharding import PartitionSpec as P

HEADS = 16
HEAD_DIM = 72


KEEP_RATE = 0.9


def project(left, right):
    flat = left.reshape(-1, left.shape[-1])
    result = jnp.dot(
        flat, right, precision=lax.Precision.HIGHEST, preferred_element_type=jnp.float32
    )
    return result.reshape(left.shape[:-1] + (right.shape[1],))


def project_back(left, right):
    flat = left.reshape(-1, left.shape[-1])
    result = lax.dot_general(
        flat,
        right,
        (((1,), (1,)), ((), ())),
        precision=lax.Precision.HIGHEST,
        preferred_element_type=jnp.float32,
    )
    return result.reshape(left.shape[:-1] + (right.shape[0],))


def outer_sum(left, right):
    flat_left = left.reshape(-1, left.shape[-1])
    flat_right = right.reshape(-1, right.shape[-1])
    return lax.dot_general(
        flat_left,
        flat_right,
        (((0,), (0,)), ((), ())),
        precision=lax.Precision.HIGHEST,
        preferred_element_type=jnp.float32,
    )


def attend(qkv_rows):
    high = lax.Precision.HIGHEST
    frames = qkv_rows.shape[1]
    patches = qkv_rows.shape[2]
    scaling = HEAD_DIM ** (-0.5)
    split = qkv_rows.reshape(frames, patches, 3, HEADS, HEAD_DIM)
    scores = jnp.einsum("fphd,gphd->phfg", split[:, :, 0], split[:, :, 1], precision=high) * scaling
    shifted = scores - jnp.max(scores, axis=-1, keepdims=True)
    expo = jnp.exp(shifted)
    attn_rows = expo / jnp.sum(expo, axis=-1, keepdims=True)
    mixed = jnp.einsum("phfg,gphd->fphd", attn_rows, split[:, :, 2], precision=high)
    return (attn_rows, mixed.reshape(1, frames, patches, HEADS * HEAD_DIM))


def attend_back(qkv_rows, attn_rows, grad_mixed):
    high = lax.Precision.HIGHEST
    frames = qkv_rows.shape[1]
    patches = qkv_rows.shape[2]
    scaling = HEAD_DIM ** (-0.5)
    split = qkv_rows.reshape(frames, patches, 3, HEADS, HEAD_DIM)
    queries = split[:, :, 0]
    key_rows = split[:, :, 1]
    value_rows = split[:, :, 2]
    grad_heads = grad_mixed.reshape(frames, patches, HEADS, HEAD_DIM)
    grad_values = jnp.einsum("phfg,fphd->gphd", attn_rows, grad_heads, precision=high)
    grad_attn = jnp.einsum("fphd,gphd->phfg", grad_heads, value_rows, precision=high)
    grad_scores = attn_rows * (grad_attn - jnp.sum(grad_attn * attn_rows, axis=-1, keepdims=True))
    grad_queries = jnp.einsum("phfg,gphd->fphd", grad_scores, key_rows, precision=high) * scaling
    grad_keys = jnp.einsum("phfg,fphd->gphd", grad_scores, queries, precision=high) * scaling
    stacked = jnp.stack([grad_queries, grad_keys, grad_values], axis=2)
    return stacked.reshape(1, frames, patches, 3 * HEADS * HEAD_DIM)


def on_device(x_saved, grad_out, keep_mask, w_qkv, w_out):
    grad_proj = grad_out * (keep_mask.astype(jnp.float32)[..., None] / KEEP_RATE)
    qkv_rows = project(x_saved, w_qkv)
    qkv_patches = lax.all_to_all(qkv_rows, "seq", split_axis=2, concat_axis=1, tiled=True)
    attn_rows, mixed_patches = attend(qkv_patches)
    mixed_frames = lax.all_to_all(mixed_patches, "seq", split_axis=1, concat_axis=2, tiled=True)
    term_out = outer_sum(mixed_frames, grad_proj)
    grad_mixed = project_back(grad_proj, w_out)
    grad_mixed_patches = lax.all_to_all(grad_mixed, "seq", split_axis=2, concat_axis=1, tiled=True)
    grad_qkv_patches = attend_back(qkv_patches, attn_rows, grad_mixed_patches)
    grad_qkv = lax.all_to_all(grad_qkv_patches, "seq", split_axis=1, concat_axis=2, tiled=True)
    term_qkv = outer_sum(x_saved, grad_qkv)
    grad_input = project_back(grad_qkv, w_qkv)
    first_qkv, first_out = (
        lax.psum_scatter(term_qkv, "seq", scatter_dimension=1, tiled=True),
        lax.psum_scatter(term_out, "seq", scatter_dimension=1, tiled=True),
    )
    total_qkv, total_out = (
        lax.psum_scatter(first_qkv, "clip", scatter_dimension=0, tiled=True),
        lax.psum_scatter(first_out, "clip", scatter_dimension=0, tiled=True),
    )
    return (grad_input, total_qkv, total_out)


def solution(mesh):
    return jax.shard_map(
        on_device,
        mesh=mesh,
        in_specs=(
            P("clip", "seq", None, None),
            P("clip", "seq", None, None),
            P("clip", "seq", None),
            P(),
            P(),
        ),
        out_specs=(P("clip", "seq", None, None), P("clip", "seq"), P("clip", "seq")),
        check_vma=False,
    )
```

profile of v0, /device:TPU:1, one launch (start us, length us, event | category | flops | bytes accessed | tf_op | source)
XLA Modules:
  0.0 636.9 jit_solution(8423254217738896385)
XLA Ops:
  8.4 19.4 %convolution_bitcast_fusion.1 = f32[1,1,256,3456]{3,2,1,0:T(8,128)S(1)} fusion(f32[1152,3456]{1,0:T(8,128)} %param.8, f32[1,1,256,1152]{3,2,1,0:T(8,128)S(1)} %copy-done), kind=kOutput, calls=%fused_computation.2 | convolution fusion | flops 12230590464 | bytes 20643840 | tf_op jit(solution)/shard_map/dot_general | solution.py:15
  31.5 59.1 %all_to_all.16 = f32[1,1,256,3456]{3,1,0,2:T(1,128)} all-to-all(f32[1,1,256,3456]{3,1,0,2:T(1,128)S(1)} %copy.38), channel_id=1, replica_groups=mesh['clip'=8,'seq'=16] {'seq'}, dimensions={2} | all-to-all | bytes 7077888 | tf_op jit(solution)/shard_map/all_to_all | solution.py:81
  90.5 11.8 %reduce = f32[256,3456]{1,0:T(8,128)} reduce(f32[1,1,256,3456]{3,1,0,2:T(1,128)} %all_to_all.16, f32[]{:T(128)} %constant.21), dimensions={0,1}, to_apply=%all_to_all.8.reduce_sub_computation | reduce | bytes 7077892 | tf_op jit(solution)/shard_map/all_to_all | solution.py:81
  102.4 8.0 %reshape.75 = f32[16,16,3,16,72]{4,3,2,1,0:T(8,128)} reshape(f32[256,3456]{1,0:T(8,128)} %reduce) | data formatting | bytes 7077888 | tf_op jit(solution)/shard_map/reshape | solution.py:64
  114.0 5.9 multiply_reduce_fusion.1
  120.8 5.0 fusion.13
  128.7 4.8 all-to-all-start.3
  133.5 17.3 %all-to-all-done.3 = f32[1,16,16,1152]{3,2,0,1:T(8,128)S(1)} async-done(((f32[1,16,16,1152]{3,2,0,1:T(8,128)}), f32[1,16,16,1152]{3,2,0,1:T(8,128)S(1)}, u32[]{:S(2)}, u32[]{:S(2)}) %all-to-all-start.3) | async-done | bytes 1179680 | tf_op jit(solution)/shard_map/all_to_all | solution.py:83
  150.8 7.2 %fusion.14 = f32[1152,1152]{0,1:T(8,128)} fusion(f32[256,1152]{1,0:T(8,128)S(1)} %bitcast.77, f32[1,1,256,1152]{3,2,1,0:T(8,128)S(1)} %copy-done.8, f32[256]{0:T(256)S(1)} %bitcast.79), kind=kOutput, calls=%fused_computation.26 | convolution fusion | flops 4077158400 | bytes 7668736 | tf_op jit(solution)/shard_map/dot_general | solution.py:36
  158.5 8.1 %convolution_bitcast_fusion.3 = f32[1,1,256,1152]{3,2,1,0:T(8,128)S(1)} fusion(f32[1152,1152]{1,0:T(8,128)} %param.9, f32[1,1,256,1152]{3,2,1,0:T(8,128)S(1)} %copy-done.8, f32[256]{0:T(256)S(1)} %bitcast.80), kind=kOutput, calls=%fused_computation.4 | convolution fusion | flops 4077158400 | bytes 7668736 | tf_op jit(solution)/shard_map/dot_general | solution.py:23
  167.9 33.4 %all_to_all.17 = f32[1,1,256,1152]{3,1,0,2:T(1,128)S(1)} all-to-all(f32[1,1,256,1152]{3,1,0,2:T(1,128)S(1)} %copy.41), channel_id=1, replica_groups=mesh['clip'=8,'seq'=16] {'seq'}, dimensions={2} | all-to-all | bytes 2359296 | tf_op jit(solution)/shard_map/all_to_all | solution.py:86
  201.2 4.1 reduce.1
  205.4 4.1 reshape.78
  209.5 5.2 fusion.10
  214.8 6.2 multiply_reduce_fusion
  224.9 4.8 multiply_bitcast_fusion.1
  230.4 4.6 copy.46
  235.0 7.0 %reshape.79 = f32[1,16,16,3456]{3,2,1,0:T(8,128)} reshape(f32[16,16,3,16,72]{4,3,2,1,0:T(8,128)} %copy.46) | data formatting | bytes 7077888 | tf_op jit(solution)/shard_map/reshape | solution.py:75
  242.0 46.6 %all_to_all.18 = f32[1,16,16,3456]{3,2,0,1:T(8,128)S(1)} all-to-all(f32[1,16,16,3456]{3,2,0,1:T(8,128)} %bitcast.76), channel_id=1, replica_groups=mesh['clip'=8,'seq'=16] {'seq'}, dimensions={1} | all-to-all | bytes 7077888 | tf_op jit(solution)/shard_map/all_to_all | solution.py:88
  290.3 17.3 %convolution_bitcast_fusion = f32[1152,3456]{0,1:T(8,128)} fusion(f32[256,3456]{1,0:T(8,128)S(1)} %bitcast.74, f32[1,1,256,1152]{3,2,1,0:T(8,128)S(1)} %copy-done), kind=kOutput, calls=%fused_computation | convolution fusion | flops 12230590464 | bytes 20643840 | tf_op jit(solution)/shard_map/dot_general | solution.py:36
  309.9 170.5 %reduce-scatter.19.cloned.1.call-done = f32[1152,216]{0,1:T(8,128)} async-done(((f32[1152,3456]{0,1:T(8,128)}), f32[1152,216]{0,1:T(8,128)}) %reduce-scatter.19.cloned.1.call-update) | async-done | bytes 995344
  483.0 20.8 %convolution_bitcast_fusion.2 = f32[1,1,256,1152]{3,2,1,0:T(8,128)} fusion(f32[256,3456]{1,0:T(8,128)} %bitcast.75, f32[1152,3456]{1,0:T(8,128)} %param.8), kind=kOutput, calls=%fused_computation.3 | convolution fusion | flops 12230590464 | bytes 20643840 | tf_op jit(solution)/shard_map/dot_general | solution.py:23
  503.7 50.6 %reduce-scatter.17.cloned.1.call-done = f32[144,72]{1,0:T(8,128)} async-done(((f32[1152,72]{1,0:T(8,128)}), f32[144,72]{1,0:T(8,128)}) %reduce-scatter.17.cloned.1.call-update) | async-done | bytes 41488
  554.4 75.5 %reduce-scatter.15.cloned.1.call-done = f32[144,216]{1,0:T(8,128)} async-done(((f32[1152,216]{1,0:T(8,128)}), f32[144,216]{1,0:T(8,128)}) %reduce-scatter.15.cloned.1.call-update) | async-done | bytes 124432
  (54 shorter events, 25.0 us)
Async XLA Ops:
  7.2 1.3 copy-start
  114.0 6.0 copy-start.4
  114.0 6.0 copy-start.6
  114.0 6.8 %copy-start.10 = (f32[16,16,1,16,72]{4,3,2,1,0:T(8,128)}, f32[16,16,1,16,72]{4,3,2,1,0:T(8,128)S(1)}, u32[]{:S(2)}) copy-start(f32[16,16,1,16,72]{4,3,2,1,0:T(8,128)S(1)} %get-tuple-element.15) | copy-start | bytes 3538948
  120.0 5.8 copy-start.2
  120.0 5.8 copy-start.12
  120.8 5.0 copy-start.14
  126.5 7.0 %copy-start.16 = (s32[1,1,256]{2,1,0:T(1,128)S(1)}, s32[1,1,256]{2,1,0:T(1,128)}, u32[]{:S(2)}) copy-start(s32[1,1,256]{2,1,0:T(1,128)} %param.7) | copy-start | bytes 3076
  128.7 22.2 %copy-start.8 = (f32[1,1,256,1152]{3,2,1,0:T(8,128)S(1)}, f32[1,1,256,1152]{3,2,1,0:T(8,128)}, u32[]{:S(2)}) copy-start(f32[1,1,256,1152]{3,2,1,0:T(8,128)} %param.6) | copy-start | bytes 3538948
  128.7 22.2 %all-to-all-start.3 = ((f32[1,16,16,1152]{3,2,0,1:T(8,128)}), f32[1,16,16,1152]{3,2,0,1:T(8,128)S(1)}, u32[]{:S(2)}, u32[]{:S(2)}) async-start(f32[1,16,16,1152]{3,2,0,1:T(8,128)} %bitcast.78), calls=%async_computation.3 | async-start | bytes 2359296 | tf_op jit(solution)/shard_map/all_to_all | solution.py:83
  133.5 174.3 %reduce-scatter.21.cloned.1.call-start = ((), (), s32[]{:S(2)}) async-start(), calls=%async_computation.11 | async-start | bytes 5640192
  158.0 322.3 %reduce-scatter.19.cloned.1.call-start = ((), (), s32[]{:S(2)}) async-start(), calls=%async_computation.10 | async-start | bytes 16920576
  205.4 4.1 copy-start.3
  205.4 4.1 copy-start.13
  205.4 4.1 copy-start.15
  209.5 5.3 copy-start.9
  209.5 5.3 copy-start.11
  214.8 6.2 copy-start.7
  221.0 3.9 copy-start.5
  288.6 1.7 copy-start.1
  307.7 246.7 %reduce-scatter.17.cloned.1.call-start = ((), (), s32[]{:S(2)}) async-start(), calls=%async_computation.9 | async-start | bytes 663552
  309.8 320.1 %reduce-scatter.15.cloned.1.call-start = ((), (), s32[]{:S(2)}) async-start(), calls=%async_computation.8 | async-start | bytes 1327104
Sparse Core Ops, SparseCore 0:
  158.1 81.8 reduce-scatter.20
  307.8 172.5 reduce-scatter.18
  484.9 69.4 reduce-scatter.16
  558.4 71.3 reduce-scatter.14
where the time goes:
time: 647 us; the launch traced here: 637 us
  waiting for transfers between devices  314 us (49%)
  blocking collectives  139 us (21%)
  matrix products  104 us (16%)
  local copies, waits for them, and re-layouts  42.6 us (7%)
  other arithmetic  17.5 us (3%)
  between operations  14.6 us (2%)
    unnamed x8, waiting for transfers between devices  297 us
    all_to_all x1, blocking collectives, on_device(): lax.all_to_all(qkv_rows, 'seq', split_axis=2, concat_axis=1, tiled=True)  59.1 us
    all_to_all x1, blocking collectives, on_device(): lax.all_to_all(grad_qkv_patches, 'seq', split_axis=1, concat_axis=2, tile...  46.6 us
    all_to_all x1, blocking collectives, on_device(): lax.all_to_all(grad_mixed, 'seq', split_axis=2, concat_axis=1, tiled=True)  33.4 us
    dot_general x2, matrix products, project_back(): lax.dot_general(flat, right, (((1,), (1,)), ((), ())), precision=lax.Prec...  28.9 us
    dot_general x2, matrix products, outer_sum(): lax.dot_general(flat_left, flat_right, (((0,), (0,)), ((), ())), precisio...  24.5 us
    dot_general x1, matrix products, project(): jnp.dot(flat, right, precision=lax.Precision.HIGHEST, preferred_element_t...  19.4 us
    all_to_all x1, waiting for transfers between devices, on_device(): lax.all_to_all(mixed_patches, 'seq', split_axis=1, concat_axis=2, tiled=T...  17.3 us
  transfers between devices with their start and end apart: 5, of which 4 were waited for; matrix products, arithmetic and copies ran while one was open for 15% of the time, Pallas kernels for 0%

commit v1 on v0

v1 whole, which is shorter than its diff:
```python
import jax
import jax.numpy as jnp
from jax import lax
from jax.sharding import PartitionSpec as P

HEADS = 16
HEAD_DIM = 72
KEEP_RATE = 0.9
HIGH = lax.Precision.HIGH


def project(left, right):
    return jnp.dot(left, right, precision=HIGH, preferred_element_type=jnp.float32)


def project_back(left, right):
    return lax.dot_general(
        left, right, (((1,), (1,)), ((), ())), precision=HIGH, preferred_element_type=jnp.float32
    )


def outer_sum(left, right):
    return lax.dot_general(
        left, right, (((0,), (0,)), ((), ())), precision=HIGH, preferred_element_type=jnp.float32
    )


def on_device(x_saved, grad_out, keep_mask, w_qkv, w_out):
    frames = lax.axis_size("seq")
    width = x_saved.shape[-1]
    patches = x_saved.shape[2] // frames
    scaling = HEAD_DIM ** (-0.5)
    grad_proj = grad_out * (keep_mask.astype(jnp.float32)[..., None] / KEEP_RATE)
    x_p = lax.all_to_all(x_saved, "seq", split_axis=2, concat_axis=1, tiled=True)
    g_p = lax.all_to_all(grad_proj, "seq", split_axis=2, concat_axis=1, tiled=True)
    x_t = x_p.reshape(-1, width)
    g_t = g_p.reshape(-1, width)
    qkv = project(x_t, w_qkv)
    split = qkv.reshape(frames, patches, 3, HEADS, HEAD_DIM)
    q, k, v = split[:, :, 0], split[:, :, 1], split[:, :, 2]
    scores = jnp.einsum("fphd,gphd->phfg", q, k, precision=HIGH) * scaling
    shifted = scores - jnp.max(scores, axis=-1, keepdims=True)
    expo = jnp.exp(shifted)
    attn = expo / jnp.sum(expo, axis=-1, keepdims=True)
    mixed = jnp.einsum("phfg,gphd->fphd", attn, v, precision=HIGH).reshape(-1, width)
    term_out = outer_sum(mixed, g_t)
    gm = project_back(g_t, w_out).reshape(frames, patches, HEADS, HEAD_DIM)
    gv = jnp.einsum("phfg,fphd->gphd", attn, gm, precision=HIGH)
    ga = jnp.einsum("fphd,gphd->phfg", gm, v, precision=HIGH)
    gs = attn * (ga - jnp.sum(ga * attn, axis=-1, keepdims=True))
    gq = jnp.einsum("phfg,gphd->fphd", gs, k, precision=HIGH) * scaling
    gk = jnp.einsum("phfg,fphd->gphd", gs, q, precision=HIGH) * scaling
    gqkv = jnp.stack([gq, gk, gv], axis=2).reshape(-1, 3 * width)
    term_qkv = outer_sum(x_t, gqkv)
    gi = project_back(gqkv, w_qkv).reshape(1, frames, patches, width)
    grad_input = lax.all_to_all(gi, "seq", split_axis=1, concat_axis=2, tiled=True)
    total_out = lax.psum_scatter(
        lax.psum_scatter(term_out, "seq", scatter_dimension=1, tiled=True), "clip", scatter_dimension=0, tiled=True
    )
    total_qkv = lax.psum_scatter(
        lax.psum_scatter(term_qkv, "seq", scatter_dimension=1, tiled=True), "clip", scatter_dimension=0, tiled=True
    )
    return (grad_input, total_qkv, total_out)


def solution(mesh):
    return jax.shard_map(
        on_device,
        mesh=mesh,
        in_specs=(
            P("clip", "seq", None, None),
            P("clip", "seq", None, None),
            P("clip", "seq", None),
            P(),
            P(),
        ),
        out_specs=(P("clip", "seq", None, None), P("clip", "seq"), P("clip", "seq")),
        check_vma=False,
    )
```

time: 647 us -> 492 us (0.76)
  blocking collectives: 139 us -> 23 us
  matrix products: 104 us -> 68.4 us
  other arithmetic: 17.5 us -> 1.66 us
  starting transfers between devices: 5.35 us -> 12.8 us
  local copies, waits for them, and re-layouts: 42.6 us -> 49.8 us
    all_to_all x3 -> x1, blocking collectives: 139 us -> 23 us  [on_device(): lax.all_to_all(gi, 'seq', split_axis=1, concat_axis=2, tiled=True)]
    dot_general x11, matrix products: 104 us -> 68.4 us  [the longest x2 18.2 us: project_back(): lax.dot_general(left, right, (((1,), (1,)), ((), ())), precision=HIGH, pr...]
    unnamed x36 -> x29, local copies, waits for them, and re-layouts: 7.71 us -> 26.6 us
    reshape x6 -> x2, local copies, waits for them, and re-layouts: 26 us -> 7.95 us  [the longest x1 5.6 us: on_device(): gqkv = jnp.stack([gq, gk, gv], axis=2).reshape(-1, 3 * width)]
    all_to_all x1 -> x2, waiting for transfers between devices: 17.3 us -> 0.01 us  [the longest x1 0.01 us: on_device(): lax.all_to_all(grad_proj, 'seq', split_axis=2, concat_axis=1, tiled=True)]
    unnamed x8, waiting for transfers between devices: 297 us -> 314 us
    all_to_all x2 -> x0, other arithmetic: 16 us -> none  [the longest x1 11.8 us: on_device(): lax.all_to_all(qkv_rows, 'seq', split_axis=2, concat_axis=1, tiled=True)]
    all_to_all x1 -> x2, starting transfers between devices: 4.79 us -> 12.6 us  [the longest x1 6.91 us: on_device(): lax.all_to_all(x_saved, 'seq', split_axis=2, concat_axis=1, tiled=True)]
  transfers between devices with their start and end apart: 5 -> 6, of which waited for: 4 -> 4; matrix products, arithmetic and copies ran while one was open for 15% -> 23% of each run, Pallas kernels for 0% -> 0%
where the time goes in v1:
time: 492 us; the launch traced here: 484 us
  waiting for transfers between devices  314 us (64%)
  matrix products  68.4 us (14%)
  local copies, waits for them, and re-layouts  49.8 us (10%)
  blocking collectives  23 us (5%)
  between operations  14.3 us (3%)
  starting transfers between devices  12.8 us (3%)
    unnamed x8, waiting for transfers between devices  314 us
    unnamed x29, local copies, waits for them, and re-layouts  26.6 us
    all_to_all x1, blocking collectives, on_device(): lax.all_to_all(gi, 'seq', split_axis=1, concat_axis=2, tiled=True)  23 us
    dot_general x2, matrix products, project_back(): lax.dot_general(left, right, (((1,), (1,)), ((), ())), precision=HIGH, pr...  18.2 us
    dot_general x2, matrix products, outer_sum(): lax.dot_general(left, right, (((0,), (0,)), ((), ())), precision=HIGH, pr...  16.8 us
    dot_general x1, matrix products, project(): jnp.dot(left, right, precision=HIGH, preferred_element_type=jnp.float32)  15.9 us
  transfers between devices with their start and end apart: 6, of which 4 were waited for; matrix products, arithmetic and copies ran while one was open for 23% of the time, Pallas kernels for 0%

profile of v1, /device:TPU:1, one launch (start us, length us, event | category | flops | bytes accessed | tf_op | source)
XLA Modules:
  0.0 483.8 jit_solution(4811021584753748985)
XLA Ops:
  7.2 3.5 copy.77
  10.7 6.9 %all-to-all-start = ((f32[1,1,256,1152]{3,1,0,2:T(1,128)}), f32[1,1,256,1152]{3,1,0,2:T(1,128)S(1)}, u32[]{:S(2)}, u32[]{:S(2)}) async-start(f32[1,1,256,1152]{3,1,0,2:T(1,128)} %copy.77), calls=%async_computation | async-start | bytes 2359296 | tf_op jit(solution)/shard_map/all_to_all | solution.py:34
  17.6 17.1 %copy.78 = f32[1152,3456]{0,1:T(8,128)} copy(f32[1152,3456]{1,0:T(8,128)} %param.8) | data formatting | bytes 31850496 | tf_op args[3]
  37.1 5.7 %all-to-all-start.1 = ((f32[1,1,256,1152]{3,1,0,2:T(1,128)}), f32[1,1,256,1152]{3,1,0,2:T(1,128)S(1)}, u32[]{:S(2)}, u32[]{:S(2)}) async-start(f32[1,1,256,1152]{3,1,0,2:T(1,128)} %copy.81), calls=%async_computation.1 | async-start | bytes 2359296 | tf_op jit(solution)/shard_map/all_to_all | solution.py:35
  43.0 15.9 %fusion.36 = f32[16,16,3,16,72]{4,1,3,2,0:T(8,128)S(1)} fusion(f32[16,16,1152,1,1]{2,1,4,3,0:T(8,128)S(1)} %bitcast.72, f32[3,16,72,1152,1]{3,2,1,0,4:T(8,128)} %bitcast.68), kind=kOutput, calls=%fused_computation.38 | convolution fusion | flops 6115295232 | bytes 20643840 | tf_op jit(solution)/shard_map/dot_general | solution.py:13
  59.7 4.2 multiply_reduce_fusion.1
  64.6 3.1 fusion.20
  69.7 2.4 reshape.62
  72.1 5.0 %fusion.25 = f32[1152,1152]{0,1:T(8,128)} fusion(f32[256,1152]{1,0:T(8,128)S(1)} %reshape.62, f32[1,1,256,1152]{3,1,0,2:T(1,128)S(1)} %all-to-all-done.1), kind=kOutput, calls=%fused_computation.29 | convolution fusion | flops 2038431744 | bytes 7667712 | tf_op jit(solution)/shard_map/dot_general | solution.py:23
  77.3 6.9 %fusion.28 = f32[16,16,16,72]{3,0,2,1:T(8,128)S(1)} fusion(f32[16,72,1152,1]{2,1,0,3:T(8,128)} %bitcast.69, f32[16,16,1152,1]{2,1,0,3:T(8,128)S(1)} %bitcast.71), kind=kOutput, calls=%fused_computation.32 | convolution fusion | flops 2038431744 | bytes 7667712 | tf_op jit(solution)/shard_map/dot_general | solution.py:17
  85.8 3.1 multiply_reduce_fusion
  88.9 3.0 multiply_bitcast_fusion.1
  92.0 2.7 multiply_bitcast_fusion
  95.4 4.8 copy.88
  100.1 5.6 %reshape.60 = f32[256,3456]{1,0:T(8,128)S(1)} reshape(f32[16,16,3,16,72]{4,3,2,1,0:T(8,128)} %copy.88) | data formatting | bytes 7077888 | tf_op jit(solution)/shard_map/reshape | solution.py:53
  105.7 11.7 %convolution_bitcast_fusion = f32[1152,3456]{0,1:T(8,128)} fusion(f32[256,3456]{1,0:T(8,128)S(1)} %reshape.60, f32[1,1,256,1152]{3,1,0,2:T(1,128)} %copy-done), kind=kOutput, calls=%fused_computation | convolution fusion | flops 6115295232 | bytes 20643840 | tf_op jit(solution)/shard_map/dot_general | solution.py:23
  117.6 32.2 %reduce-scatter.21.cloned.1.call-done = f32[1152,72]{0,1:T(8,128)} async-done(((f32[1152,1152]{0,1:T(8,128)}), f32[1152,72]{0,1:T(8,128)}) %reduce-scatter.21.cloned.1.call-update) | async-done | bytes 331792
  151.9 5.6 %reshape.59 = f32[16,16,3456]{2,1,0:T(8,128)S(1)} reshape(f32[16,16,3,16,72]{4,3,2,1,0:T(8,128)} %copy.88) | data formatting | bytes 7077888 | tf_op jit(solution)/shard_map/reshape.36
  157.5 168.7 %reduce-scatter.19.cloned.1.call-done = f32[1152,216]{0,1:T(8,128)} async-done(((f32[1152,3456]{0,1:T(8,128)}), f32[1152,216]{0,1:T(8,128)}) %reduce-scatter.19.cloned.1.call-update) | async-done | bytes 995344
  326.2 2.6 copy.101
  328.8 11.3 %fusion.2 = f32[1,16,16,1152]{3,2,0,1:T(8,128)S(1)} fusion(f32[16,16,3456]{2,1,0:T(8,128)S(1)} %reshape.59, f32[1152,3456]{1,0:T(8,128)} %param.8), kind=kOutput, calls=%fused_computation.4 | convolution fusion | flops 6115295232 | bytes 20643840 | tf_op jit(solution)/shard_map/dot_general | solution.py:17
  340.2 23.0 %all_to_all.30 = f32[1,16,16,1152]{3,2,0,1:T(8,128)S(1)} all-to-all(f32[1,16,16,1152]{3,2,0,1:T(8,128)S(1)} %fusion.2), channel_id=1, replica_groups=mesh['clip'=8,'seq'=16] {'seq'}, dimensions={1} | all-to-all | bytes 2359296 | tf_op jit(solution)/shard_map/all_to_all | solution.py:56
  363.2 37.4 %reduce-scatter.17.cloned.1.call-done = f32[144,72]{1,0:T(8,128)} async-done(((f32[1152,72]{1,0:T(8,128)}), f32[144,72]{1,0:T(8,128)}) %reduce-scatter.17.cloned.1.call-update) | async-done | bytes 41488
  400.5 75.5 %reduce-scatter.15.cloned.1.call-done = f32[144,216]{1,0:T(8,128)} async-done(((f32[1152,216]{1,0:T(8,128)}), f32[144,216]{1,0:T(8,128)}) %reduce-scatter.15.cloned.1.call-update) | async-done | bytes 124432
  (44 shorter events, 11.6 us)
Async XLA Ops:
  10.7 26.5 %all-to-all-start = ((f32[1,1,256,1152]{3,1,0,2:T(1,128)}), f32[1,1,256,1152]{3,1,0,2:T(1,128)S(1)}, u32[]{:S(2)}, u32[]{:S(2)}) async-start(f32[1,1,256,1152]{3,1,0,2:T(1,128)} %copy.77), calls=%async_computation | async-start | bytes 2359296 | tf_op jit(solution)/shard_map/all_to_all | solution.py:34
  17.6 17.2 %copy-start.10 = (s32[1,1,256]{2,1,0:T(1,128)S(1)}, s32[1,1,256]{2,1,0:T(1,128)}, u32[]{:S(2)}) copy-start(s32[1,1,256]{2,1,0:T(1,128)} %param.7) | copy-start | bytes 3076
  17.6 17.2 %copy-start.9 = (f32[1,1,256,1152]{3,2,1,0:T(8,128)S(1)}, f32[1,1,256,1152]{3,2,1,0:T(8,128)}, u32[]{:S(2)}) copy-start(f32[1,1,256,1152]{3,2,1,0:T(8,128)} %param.6) | copy-start | bytes 3538948
  37.1 5.9 %copy-start = (f32[1,1,256,1152]{3,1,0,2:T(1,128)}, f32[1,1,256,1152]{3,1,0,2:T(1,128)S(1)}, u32[]{:S(2)}) copy-start(f32[1,1,256,1152]{3,1,0,2:T(1,128)S(1)} %all-to-all-done) | copy-start | bytes 3538948
  37.1 35.0 %all-to-all-start.1 = ((f32[1,1,256,1152]{3,1,0,2:T(1,128)}), f32[1,1,256,1152]{3,1,0,2:T(1,128)S(1)}, u32[]{:S(2)}, u32[]{:S(2)}) async-start(f32[1,1,256,1152]{3,1,0,2:T(1,128)} %copy.81), calls=%async_computation.1 | async-start | bytes 2359296 | tf_op jit(solution)/shard_map/all_to_all | solution.py:35
  42.9 106.9 %reduce-scatter.21.cloned.1.call-start = ((), (), s32[]{:S(2)}) async-start(), calls=%async_computation.10 | async-start | bytes 5640192
  59.6 4.2 copy-start.3
  59.6 4.2 copy-start.5
  59.6 5.0 %copy-start.7 = (f32[16,16,16,72]{3,1,2,0:T(8,128)}, f32[16,16,16,72]{3,1,2,0:T(8,128)S(1)}, u32[]{:S(2)}) copy-start(f32[16,16,16,72]{3,1,2,0:T(8,128)S(1)} %get-tuple-element.18) | copy-start | bytes 3538948
  63.8 3.9 copy-start.1
  77.2 249.0 %reduce-scatter.19.cloned.1.call-start = ((), (), s32[]{:S(2)}) async-start(), calls=%async_computation.9 | async-start | bytes 16920576
  77.3 6.9 %copy-start.2 = (f32[16,16,16,16]{2,3,1,0:T(8,128)S(1)}, f32[16,16,16,16]{2,3,1,0:T(8,128)}, u32[]{:S(2)}) copy-start(f32[16,16,16,16]{2,3,1,0:T(8,128)} %copy-done.1) | copy-start | bytes 786436
  84.2 1.6 copy-start.8
  85.8 3.1 copy-start.6
  88.9 3.1 copy-start.4
  117.5 283.0 %reduce-scatter.17.cloned.1.call-start = ((), (), s32[]{:S(2)}) async-start(), calls=%async_computation.8 | async-start | bytes 663552
  151.9 324.2 %reduce-scatter.15.cloned.1.call-start = ((), (), s32[]{:S(2)}) async-start(), calls=%async_computation.7 | async-start | bytes 1327104
Sparse Core Ops, SparseCore 0:
  77.3 72.4 reduce-scatter.20
  152.2 173.9 reduce-scatter.18
  330.8 69.7 reduce-scatter.16
  404.6 71.4 reduce-scatter.14

commit v2 on v1

v2 whole, which is shorter than its diff:
```python
import jax
import jax.numpy as jnp
from jax import lax
from jax.experimental import pallas as pl
from jax.experimental.pallas import tpu as pltpu
from jax.sharding import PartitionSpec as P

HEADS = 16
HEAD_DIM = 72
KEEP_RATE = 0.9
D = 1152
LOCAL = 8
PART = 640
ROWS = 120
MESH = pl.DeviceIdType.MESH
F32 = jnp.float32
BF16 = jnp.bfloat16

NN = (((1,), (0,)), ((), ()))
NT = (((1,), (1,)), ((), ()))


def split(value):
    high = value.astype(BF16)
    return high, (value - high.astype(F32)).astype(BF16)


def dot(left, right, dims):
    return lax.dot_general(left, right, dims, preferred_element_type=F32)


def dot3(left_high, left_low, right_high, right_low, dims):
    return (
        dot(left_high, right_high, dims)
        + dot(left_low, right_high, dims)
        + dot(left_high, right_low, dims)
    )


def iota(shape, dim):
    return lax.broadcasted_iota(jnp.int32, shape, dim)


def wait_copy(ref, sem):
    pltpu.make_async_copy(ref, ref, sem).wait()


def compute_kernel(
    x_hbm, g_hbm, mask_ref, wqkv_hbm, wout_hbm, gw_hbm, gi_hbm,
    xl, gl, gsrc, wst, sel, wph, wpl, woh, wol, xth, xtl, qkv, gqkv, gm, mixed, mth, mtl,
    gph, gpl, big_h, big_l, gqh, gql, outw, gwbuf, gibuf,
    xs_sem, xr_sem, xfs_sem, xfr_sem, gs_sem, gr_sem, gfs_sem, gfr_sem, loc_sem, w_sem, gw_sem,
):
    clip = lax.axis_index("clip")
    seq = lax.axis_index("seq")
    chip = seq // 2
    core = seq % 2
    sibling = (clip, 2 * chip + 1 - core)

    def peer(d):
        return (clip, 2 * ((chip + d) % 8) + core)

    def frame_from(d, c):
        return 2 * ((chip + 8 - d) % 8) + c

    barrier = pltpu.get_barrier_semaphore()
    for d in range(1, 8):
        pl.semaphore_signal(barrier, inc=1, device_id=peer(d), device_id_type=MESH)
    pl.semaphore_signal(barrier, inc=1, device_id=sibling, device_id_type=MESH)

    own_frame = 2 * chip + core
    load_x = pltpu.make_async_copy(x_hbm.at[chip], xl.at[:, own_frame], loc_sem.at[0])
    load_x.start()
    load_g = pltpu.make_async_copy(g_hbm, gsrc, loc_sem.at[1])
    load_g.start()

    def weight_copy(step, slot):
        return pltpu.make_async_copy(
            wqkv_hbm.at[pl.ds(step * 144, 144)], wst.at[slot], w_sem.at[slot]
        )

    weight_copy(0, 0).start()
    pl.semaphore_wait(barrier, 8)

    def send(src, dst, send_sems, recv_sems, d):
        p = (chip + d) % 8
        return pltpu.make_async_remote_copy(
            src_ref=src.at[p],
            dst_ref=dst.at[:, own_frame],
            send_sem=send_sems.at[d],
            recv_sem=recv_sems.at[d],
            device_id=peer(d),
            device_id_type=MESH,
        )

    def arrival(dst, send_sems, recv_sems, d):
        view = dst.at[:, frame_from(d, core)]
        return pltpu.make_async_remote_copy(
            src_ref=view, dst_ref=view, send_sem=send_sems.at[d], recv_sem=recv_sems.at[d],
            device_id=peer(d), device_id_type=MESH,
        )

    def forward(dst, send_sems, recv_sems, d):
        view = dst.at[:, frame_from(d, core)]
        return pltpu.make_async_remote_copy(
            src_ref=view, dst_ref=view, send_sem=send_sems.at[d], recv_sem=recv_sems.at[d],
            device_id=sibling, device_id_type=MESH,
        )

    def forwarded(dst, send_sems, recv_sems, d):
        view = dst.at[:, frame_from(d, 1 - core)]
        return pltpu.make_async_remote_copy(
            src_ref=view, dst_ref=view, send_sem=send_sems.at[d], recv_sem=recv_sems.at[d],
            device_id=sibling, device_id_type=MESH,
        )

    for d in range(1, 8):
        send(x_hbm, xl, xs_sem, xr_sem, d).start()

    load_g.wait()
    same = iota((256, 256), 0) == iota((256, 256), 1)
    keep = mask_ref[...].astype(F32)
    column = jnp.sum(jnp.where(same, keep, 0.0), axis=1, keepdims=True) / KEEP_RATE
    column = column.reshape(8, 4, 8, 1)
    for p in range(8):
        gsrc[p] = gsrc[p] * column[p]

    bases = (0, 128, 384, 640, 640)
    for n in range(5):
        lane = iota((512, 128), 1) + 128 * n
        head = lane // HEAD_DIM
        source = lane + HEAD_DIM * (head + core) - bases[n]
        hit = (iota((512, 128), 0) == source) & (lane < LOCAL * HEAD_DIM)
        sel[n] = jnp.where(hit, 1.0, 0.0).astype(BF16)

    load_x.wait()
    forward(xl, xfs_sem, xfr_sem, 0).start()

    def prepare(step, carry):
        slot = step % 2

        @pl.when(step < 7)
        def _():
            weight_copy(step + 1, 1 - slot).start()

        weight_copy(step, slot).wait()
        rows = pl.ds(pl.multiple_of(step * 144, 16), 144)
        for part in range(3):
            for n in range(5):
                first = D * part + bases[n]
                high, low = split(wst[slot, :, first : first + 512])
                to = pl.ds(PART * part + 128 * n, 128)
                wph[rows, to] = dot(high, sel[n], NN).astype(BF16)
                wpl[rows, to] = dot(low, sel[n], NN).astype(BF16)
        return carry

    lax.fori_loop(0, 8, prepare, 0)

    def head_copy(a):
        return pltpu.make_async_copy(
            wout_hbm.at[pl.ds(HEAD_DIM * (2 * a + core), HEAD_DIM)],
            outw.at[pl.ds(HEAD_DIM * a, HEAD_DIM)],
            w_sem.at[2 + a],
        )

    for a in range(LOCAL):
        head_copy(a).start()

    for d in range(1, 8):
        arrival(xl, xs_sem, xr_sem, d).wait_recv()
        forward(xl, xfs_sem, xfr_sem, d).start()
    for d in range(1, 8):
        send(x_hbm, xl, xs_sem, xr_sem, d).wait_send()
    for d in range(1, 8):
        send(gsrc, gl, gs_sem, gr_sem, d).start()
    own_g = pltpu.make_async_copy(gsrc.at[chip], gl.at[:, own_frame], loc_sem.at[2])
    own_g.start()

    for a in range(LOCAL):
        head_copy(a).wait()
    for n in range(4):
        high, low = split(outw[144 * n : 144 * n + 144, :])
        woh[144 * n : 144 * n + 144, :] = high
        wol[144 * n : 144 * n + 144, :] = low
    woh[576:640, :] = jnp.zeros((64, D), BF16)
    wol[576:640, :] = jnp.zeros((64, D), BF16)

    for d in range(8):
        forwarded(xl, xfs_sem, xfr_sem, d).wait_recv()
    own_g.wait()
    forward(gl, gfs_sem, gfr_sem, 0).start()

    def split_rows(src, high_ref, low_ref, turn):
        def body(g, carry):
            rows = pl.ds(pl.multiple_of(g * 128, 128), 128)
            value = src[g].reshape(128, D)
            high, low = split(value)
            high_ref[rows, 0:D] = high
            low_ref[rows, 0:D] = low
            if turn:
                high, low = split(value.T)
                xth[:, rows] = high
                xtl[:, rows] = low
            return carry

        lax.fori_loop(0, 4, body, 0)

    split_rows(xl, big_h, big_l, True)

    def project(first, width):
        to = pl.ds(first, width)
        qkv[:, to] = dot3(
            big_h[:, 0:D], big_l[:, 0:D], wph[:, to], wpl[:, to], NN
        )

    def project_tile(n, carry):
        project(pl.multiple_of(n * 256, 256), 256)
        return carry

    lax.fori_loop(0, 7, project_tile, 0)
    project(1792, 128)

    for d in range(1, 8):
        arrival(gl, gs_sem, gr_sem, d).wait_recv()
        forward(gl, gfs_sem, gfr_sem, d).start()
    for part in range(3):
        gqkv[:, PART * part + 512 : PART * part + 640] = jnp.zeros((512, 128), F32)
    mixed[:, 512:640] = jnp.zeros((512, 128), F32)
    for d in range(8):
        forwarded(gl, gfs_sem, gfr_sem, d).wait_recv()
    split_rows(gl, gqh, gql, False)

    for first, width in ((0, 256), (256, 256), (512, 128)):
        gm[:, first : first + width] = dot3(
            gqh[:, 0:D], gql[:, 0:D], woh[first : first + width, :], wol[first : first + width, :], NT
        )

    def regroup(g, carry):
        rows = pl.ds(pl.multiple_of(g * 128, 128), 128)
        value = gl[g].reshape(128, D)
        lane = iota((128, 128), 1)
        rest = value[:, 128:256]
        for j in range(8):
            tile = 144 * j // 128
            offset = 144 * j % 128
            if offset:
                window = value[:, 128 * tile : 128 * tile + 256]
                piece = pltpu.roll(window, 256 - offset, 1)[:, 0:128]
            else:
                piece = value[:, 128 * tile : 128 * tile + 128]
            high, low = split(piece)
            gph[rows, 128 * j : 128 * j + 128] = high
            gpl[rows, 128 * j : 128 * j + 128] = low
            if j:
                rest = jnp.where(lane // 16 == j, value[:, 128 * (j + 1) : 128 * (j + 2)], rest)
        high, low = split(rest)
        gph[rows, 1024:1152] = high
        gpl[rows, 1024:1152] = low
        return carry

    lax.fori_loop(0, 4, regroup, 0)

    scaling = HEAD_DIM ** (-0.5)

    def attend(g, carry):
        rows = pl.ds(pl.multiple_of(g * 128, 128), 128)
        same_patch = (iota((128, 128), 0) % 8) == (iota((128, 128), 1) % 8)
        lane = iota((128, 256), 1)
        for a in range(LOCAL):
            first = min(HEAD_DIM * a // 128 * 128, 384)
            low_lane = HEAD_DIM * a - first
            mine = (lane >= low_lane) & (lane < low_lane + HEAD_DIM)
            q = jnp.where(mine, qkv[rows, first : first + 256], 0.0) * scaling
            qh, ql = split(q)
            kh, kl = split(qkv[rows, PART + first : PART + first + 256])
            vh, vl = split(qkv[rows, 2 * PART + first : 2 * PART + first + 256])
            mh, ml = split(jnp.where(mine, gm[rows, first : first + 256], 0.0))
            scores = jnp.where(same_patch, dot3(qh, ql, kh, kl, NT), -1e30)
            expo = jnp.exp(scores - jnp.max(scores, axis=1, keepdims=True))
            attn = expo / jnp.sum(expo, axis=1, keepdims=True)
            ah, al = split(attn)
            grad_attn = dot3(mh, ml, vh, vl, NT)
            grad_scores = attn * (grad_attn - jnp.sum(grad_attn * attn, axis=1, keepdims=True))
            sh, sl = split(grad_scores)
            th, tl = split(attn.T)
            uh, ul = split(grad_scores.T)

            def put(ref, start, value):
                pltpu.store(ref.at[rows, start + first : start + first + 256], value, mask=mine)

            put(mixed, 0, dot3(ah, al, vh, vl, NN))
            put(gqkv, 0, dot3(sh, sl, kh, kl, NN) * scaling)
            put(gqkv, PART, dot3(uh, ul, qh, ql, NN))
            put(gqkv, 2 * PART, dot3(th, tl, mh, ml, NN))
        return carry

    lax.fori_loop(0, 4, attend, 0)

    def arrange(g, carry):
        rows = pl.ds(pl.multiple_of(g * 128, 128), 128)
        high, low = split(gqkv[rows, :])
        gqh[rows, :] = high
        gql[rows, :] = low
        lane = iota((128, 256), 1)
        for j in range(8):
            starts = [PART * ((3 * j + k) // 8) + HEAD_DIM * ((3 * j + k) % 8) for k in range(3)]
            base = starts[0] // 128 * 128
            end = -(-(starts[2] + HEAD_DIM) // 128) * 128
            window = gqkv[rows, base:end]
            value = jnp.zeros((128, 256), F32)
            done = {}
            for k in range(3):
                shift = (starts[k] - base - HEAD_DIM * k) % (end - base)
                if shift not in done:
                    moved = window if shift == 0 else pltpu.roll(window, end - base - shift, 1)
                    done[shift] = moved[:, 0:256]
                value = jnp.where((lane >= HEAD_DIM * k) & (lane < HEAD_DIM * k + HEAD_DIM), done[shift], value)
            high, low = split(value)
            big_h[rows, 256 * j : 256 * j + 256] = high
            big_l[rows, 256 * j : 256 * j + 256] = low
        high, low = split(mixed[rows, :].T)
        mth[:, rows] = high
        mtl[:, rows] = low
        return carry

    lax.fori_loop(0, 4, arrange, 0)

    def out_tile(first, width):
        to = pl.ds(first, width)
        outw[:, to] = dot3(mth[...], mtl[...], gph[:, to], gpl[:, to], NN)[0:576]

    def out_step(n, carry):
        out_tile(pl.multiple_of(n * 256, 256), 256)
        return carry

    lax.fori_loop(0, 4, out_step, 0)
    out_tile(1024, 128)

    def gw_copies(j, slot):
        dy = j // 2
        dx_low = j % 2
        copies = []
        for dx_high in range(2):
            dx = 2 * dx_high + dx_low
            for t, target in enumerate(
                (gw_hbm.at[0, dx, dy], gw_hbm.at[1, dy, :, dx], gw_hbm.at[2, :, dx, dy])
            ):
                copies.append(
                    pltpu.make_async_copy(
                        gwbuf.at[slot, t, dx_high], target, gw_sem.at[slot, 3 * dx_high + t]
                    )
                )
        return copies

    def gw_step(j, carry):
        slot = j % 2

        @pl.when(j >= 2)
        def _():
            for copy in gw_copies(j - 2, slot):
                copy.wait()

        to = pl.ds(pl.multiple_of(j * 256, 256), 256)
        rest = pltpu.roll(outw[:, 1024:1152], (88 + 128 - 16 * j) % 128, 1)
        lane = iota((24, 128), 1)
        inside = (lane >= 88) & (lane < 104)
        main = pl.ds(pl.multiple_of(j * 128, 128), 128)
        term = dot3(xth[...], xtl[...], big_h[:, to], big_l[:, to], NN)
        for i in range(8):
            dz, dx_high = i // 2, i % 2
            for t in range(3):
                row = 144 * i + 48 * t
                gwbuf[slot, t, dx_high, dz, 0:48, :] = term[row : row + 48, 0:128]
                second = term[row : row + 48, 128:256]
                out_row = HEAD_DIM * i + 24 * t
                gwbuf[slot, t, dx_high, dz, 48:72, :] = jnp.where(
                    inside, rest[out_row : out_row + 24], second[0:24]
                )
                gwbuf[slot, t, dx_high, dz, 72:96, :] = second[24:48]
                gwbuf[slot, t, dx_high, dz, 96:120, :] = outw[out_row : out_row + 24, main]
        for copy in gw_copies(j, slot):
            copy.start()
        return carry

    lax.fori_loop(0, 8, gw_step, 0)

    def input_tile(first, width):
        to = pl.ds(first, width)
        term = dot3(gqh[...], gql[...], wph[to, :], wpl[to, :], NT)
        gibuf[:, :, :, to] = term.reshape(4, 16, 8, width)

    def input_step(n, carry):
        input_tile(pl.multiple_of(n * 256, 256), 256)
        return carry

    lax.fori_loop(0, 4, input_step, 0)
    input_tile(1024, 128)
    store = pltpu.make_async_copy(gibuf, gi_hbm, loc_sem.at[3])
    store.start()
    for d in range(1, 8):
        send(gsrc, gl, gs_sem, gr_sem, d).wait_send()
    for d in range(8):
        forward(xl, xfs_sem, xfr_sem, d).wait_send()
        forward(gl, gfs_sem, gfr_sem, d).wait_send()
    for j in (6, 7):
        for copy in gw_copies(j, j % 2):
            copy.wait()
    store.wait()


def exchange_kernel(
    gw_hbm, gi_hbm, input_out, qkv_out, out_out,
    one1, two1, load1, own1, one2, two2, own2, one3, two3, own3, last, other, gi_own, gi_recv,
    rs_send, rs_recv, ld_sem, gi_ld, gx_send, gx_recv, ga_send, ga_recv, fin_sem,
):
    clip = lax.axis_index("clip")
    seq = lax.axis_index("seq")
    chip = seq // 2
    core = seq % 2
    sibling = (clip, 2 * chip + 1 - core)
    here = (2 * (clip % 2) + chip % 2, chip // 2, clip // 2)

    def at(x, y, z):
        return (2 * z + x // 2, 4 * y + 2 * (x % 2) + core)

    def along(axis, step):
        place = list(here)
        place[axis] = (place[axis] + step + 4) % 4
        return at(*place)

    def peer(d):
        return (clip, 2 * ((chip + d) % 8) + core)

    barrier = pltpu.get_barrier_semaphore()
    for axis in range(3):
        for step in (1, -1):
            pl.semaphore_signal(barrier, inc=1, device_id=along(axis, step), device_id_type=MESH)
    for d in range(1, 8):
        pl.semaphore_signal(barrier, inc=1, device_id=peer(d), device_id_type=MESH)
    pl.semaphore_signal(barrier, inc=1, device_id=sibling, device_id_type=MESH)

    orders = ((0, 1, 2), (1, 2, 0), (2, 0, 1))
    ones = (one1, one2, one3)
    twos = (two1, two2, two3)
    halves = (((0, 2), (2, 2)), ((0, 2), (2, 2)), ((0, 64), (64, 56)))

    def spots(t, stage):
        me = here[orders[t][stage]]
        return me, (me + 1) % 4, (me + 3) % 4, (me + 2) % 4

    def source(t, stage, spot, half):
        start, size = halves[stage][half]
        ref = (gw_hbm, own1, own2)[stage]
        return ref.at[t, spot, pl.ds(start, size)]

    def first_hop(t, stage, half):
        me, up, down, far = spots(t, stage)
        start, size = halves[stage][half]
        return pltpu.make_async_remote_copy(
            src_ref=source(t, stage, far, half),
            dst_ref=ones[stage].at[t, half, pl.ds(0, size)],
            send_sem=rs_send.at[t, stage, half],
            recv_sem=rs_recv.at[t, stage, half],
            device_id=along(orders[t][stage], 1 if half == 0 else -1),
            device_id_type=MESH,
        )

    def second_hop(t, stage, way, half):
        me, up, down, far = spots(t, stage)
        start, size = halves[stage][half]
        if half == way:
            src = ones[stage].at[t, half, pl.ds(0, size)]
        else:
            src = source(t, stage, up if way == 0 else down, half)
        slot = 2 + 2 * way + half
        return pltpu.make_async_remote_copy(
            src_ref=src,
            dst_ref=twos[stage].at[t, way, pl.ds(start, size)],
            send_sem=rs_send.at[t, stage, slot],
            recv_sem=rs_recv.at[t, stage, slot],
            device_id=along(orders[t][stage], 1 if way == 0 else -1),
            device_id_type=MESH,
        )

    def local_loads(t):
        me, up, down, far = spots(t, 0)
        return (
            pltpu.make_async_copy(source(t, 0, up, 0), load1.at[t, 0], ld_sem.at[t, 0]),
            pltpu.make_async_copy(source(t, 0, down, 1), load1.at[t, 1], ld_sem.at[t, 1]),
            pltpu.make_async_copy(gw_hbm.at[t, me], own1.at[t], ld_sem.at[t, 2]),
        )

    def gi_load(p):
        return pltpu.make_async_copy(gi_hbm.at[:, 2 * p + core], gi_own.at[p], gi_ld.at[p])

    def gi_cross(p):
        return pltpu.make_async_remote_copy(
            src_ref=gi_hbm.at[:, 2 * p + 1 - core],
            dst_ref=gi_recv.at[p],
            send_sem=gx_send.at[p],
            recv_sem=gx_recv.at[p],
            device_id=sibling,
            device_id_type=MESH,
        )

    def gi_back(d):
        return pltpu.make_async_remote_copy(
            src_ref=gi_own.at[(chip + d) % 8],
            dst_ref=input_out.at[chip],
            send_sem=ga_send.at[d],
            recv_sem=ga_recv.at[d],
            device_id=peer(d),
            device_id_type=MESH,
        )

    def gi_arrival(d):
        view = input_out.at[(chip + 8 - d) % 8]
        return pltpu.make_async_remote_copy(
            src_ref=view, dst_ref=view, send_sem=ga_send.at[d], recv_sem=ga_recv.at[d],
            device_id=peer(d), device_id_type=MESH,
        )

    for t in range(3):
        for copy in local_loads(t):
            copy.start()
    for p in range(8):
        gi_load(p).start()
    pl.semaphore_wait(barrier, 14)

    def open_stage(stage):
        for half in range(2):
            for t in range(3):
                first_hop(t, stage, half).start()
        for way in range(2):
            for t in range(3):
                second_hop(t, stage, way, 1 - way).start()

    def middle(stage):
        for t in range(3):
            for way in range(2):
                first_hop(t, stage, way).wait_recv()
                start, size = halves[stage][way]
                me, up, down, far = spots(t, stage)
                to = ones[stage].at[t, way, pl.ds(0, size)]
                if stage == 0:
                    to[...] = to[...] + load1[t, way]
                else:
                    to[...] = to[...] + source(t, stage, up if way == 0 else down, way)[...]
                second_hop(t, stage, way, way).start()

    def close_stage(stage):
        for t in range(3):
            me, up, down, far = spots(t, stage)
            for way in range(2):
                for half in range(2):
                    second_hop(t, stage, way, half).wait_recv()
            if stage == 0:
                own1[t] = own1[t] + two1[t, 0] + two1[t, 1]
            elif stage == 1:
                own2[t] = own1[t, me] + two2[t, 0] + two2[t, 1]
            else:
                last[t] = own2[t, me] + two3[t, 0] + two3[t, 1]

    open_stage(0)
    for p in range(8):
        gi_cross(p).start()
    for t in range(3):
        for copy in local_loads(t):
            copy.wait()
    for d in range(8):
        p = (chip + d) % 8
        gi_load(p).wait()
        gi_cross(p).wait_recv()
        gi_own[p] = gi_own[p] + gi_recv[p]
        if d:
            gi_back(d).start()
    keep = pltpu.make_async_copy(gi_own.at[chip], input_out.at[chip], fin_sem.at[0])
    keep.start()
    middle(0)
    close_stage(0)
    open_stage(1)
    middle(1)
    close_stage(1)
    open_stage(2)
    middle(2)
    close_stage(2)

    swap = pltpu.make_async_remote_copy(
        src_ref=last, dst_ref=other, send_sem=fin_sem.at[1], recv_sem=fin_sem.at[2],
        device_id=sibling, device_id_type=MESH,
    )
    swap.start()
    swap.wait_recv()

    lane = iota((48, 256), 1)
    even = core == 0
    lane_out = iota((24, 128), 1)
    for t in range(3):
        mine = jnp.concatenate([last[t, 0:48, :], last[t, 48:96, :]], axis=1)
        yours = jnp.concatenate([other[t, 0:48, :], other[t, 48:96, :]], axis=1)
        turned = jnp.where(even, pltpu.roll(mine, HEAD_DIM, 1), pltpu.roll(mine, 256 - HEAD_DIM, 1))
        middle_part = jnp.where(even, pltpu.roll(yours, HEAD_DIM, 1), pltpu.roll(yours, 256 - HEAD_DIM, 1))
        left = jnp.where(even, mine, turned)
        right = jnp.where(even, turned, mine)
        whole = jnp.where(lane < HEAD_DIM, left, jnp.where(lane < 2 * HEAD_DIM, middle_part, right))
        qkv_out[48 * t : 48 * t + 48, :] = whole[:, 0:216]

        def out_rows(ref):
            main = ref[t, 96:120, :]
            rest = pltpu.roll(ref[t, 48:72, :], 128 - 32, 1)
            moved = jnp.where(lane_out < 56, pltpu.roll(main, 128 - HEAD_DIM, 1), rest)
            return jnp.where(even, main, moved)

        a = out_rows(last)
        b = out_rows(other)
        out_out[24 * t : 24 * t + 24, :] = jnp.where(even, a, b)[:, 0:HEAD_DIM]
        out_out[72 + 24 * t : 96 + 24 * t, :] = jnp.where(even, b, a)[:, 0:HEAD_DIM]

    for d in range(1, 8):
        gi_arrival(d).wait_recv()
        gi_back(d).wait_send()
    for p in range(8):
        gi_cross(p).wait_send()
    for stage in range(3):
        for t in range(3):
            for half in range(2):
                first_hop(t, stage, half).wait_send()
                for way in range(2):
                    second_hop(t, stage, way, half).wait_send()
    swap.wait_send()
    keep.wait()


def on_device(x_saved, grad_out, keep_mask, w_qkv, w_out):
    any_space = pl.BlockSpec(memory_space=pl.ANY)
    in_vmem = pl.BlockSpec(memory_space=pltpu.VMEM)
    dma = pltpu.SemaphoreType.DMA
    shape = jax.ShapeDtypeStruct
    vmem = pltpu.VMEM
    gw, gi = pl.pallas_call(
        compute_kernel,
        out_shape=(shape((3, 4, 4, 4, ROWS, 128), F32), shape((4, 16, 8, D), F32)),
        in_specs=[any_space, any_space, in_vmem, any_space, any_space],
        out_specs=(any_space, any_space),
        scratch_shapes=[
            vmem((4, 16, 8, D), F32),
            vmem((4, 16, 8, D), F32),
            vmem((8, 4, 8, D), F32),
            vmem((2, 144, 3 * D), F32),
            vmem((5, 512, 128), BF16),
            vmem((D, 3 * PART), BF16),
            vmem((D, 3 * PART), BF16),
            vmem((PART, D), BF16),
            vmem((PART, D), BF16),
            vmem((D, 512), BF16),
            vmem((D, 512), BF16),
            vmem((512, 3 * PART), F32),
            vmem((512, 3 * PART), F32),
            vmem((512, PART), F32),
            vmem((512, PART), F32),
            vmem((PART, 512), BF16),
            vmem((PART, 512), BF16),
            vmem((512, D), BF16),
            vmem((512, D), BF16),
            vmem((512, 2048), BF16),
            vmem((512, 2048), BF16),
            vmem((512, 3 * PART), BF16),
            vmem((512, 3 * PART), BF16),
            vmem((576, D), F32),
            vmem((2, 3, 2, 4, ROWS, 128), F32),
            vmem((4, 16, 8, D), F32),
            dma((8,)), dma((8,)), dma((8,)), dma((8,)),
            dma((8,)), dma((8,)), dma((8,)), dma((8,)),
            dma((4,)), dma((10,)), dma((2, 6)),
        ],
        compiler_params=pltpu.CompilerParams(
            collective_id=0, has_side_effects=True, vmem_limit_bytes=62 * 2**20
        ),
        cost_estimate=pl.CostEstimate(flops=23 * 10**9, bytes_accessed=40 * 10**6, transcendentals=10**6),
    )(
        x_saved.reshape(8, 4, 8, D),
        grad_out.reshape(8, 4, 8, D),
        keep_mask.reshape(1, 256),
        w_qkv,
        w_out,
    )
    grad_input, total_qkv, total_out = pl.pallas_call(
        exchange_kernel,
        out_shape=(shape((8, 4, 8, D), F32), shape((144, 216), F32), shape((144, 72), F32)),
        in_specs=[any_space, any_space],
        out_specs=(any_space, in_vmem, in_vmem),
        scratch_shapes=[
            vmem((3, 2, 2, 4, ROWS, 128), F32),
            vmem((3, 2, 4, 4, ROWS, 128), F32),
            vmem((3, 2, 2, 4, ROWS, 128), F32),
            vmem((3, 4, 4, ROWS, 128), F32),
            vmem((3, 2, 2, ROWS, 128), F32),
            vmem((3, 2, 4, ROWS, 128), F32),
            vmem((3, 4, ROWS, 128), F32),
            vmem((3, 2, 64, 128), F32),
            vmem((3, 2, ROWS, 128), F32),
            vmem((3, ROWS, 128), F32),
            vmem((3, ROWS, 128), F32),
            vmem((3, ROWS, 128), F32),
            vmem((8, 4, 8, D), F32),
            vmem((8, 4, 8, D), F32),
            dma((3, 3, 6)), dma((3, 3, 6)), dma((3, 3)), dma((8,)),
            dma((8,)), dma((8,)), dma((8,)), dma((8,)), dma((3,)),
        ],
        compiler_params=pltpu.CompilerParams(
            collective_id=1, has_side_effects=True, vmem_limit_bytes=48 * 2**20
        ),
        cost_estimate=pl.CostEstimate(flops=10**7, bytes_accessed=40 * 10**6, transcendentals=0),
    )(gw, gi)
    return (grad_input.reshape(1, 1, 256, D), total_qkv, total_out)


def solution(mesh):
    return jax.shard_map(
        on_device,
        mesh=mesh,
        in_specs=(
            P("clip", "seq", None, None),
            P("clip", "seq", None, None),
            P("clip", "seq", None),
            P(),
            P(),
        ),
        out_specs=(P("clip", "seq", None, None), P("clip", "seq"), P("clip", "seq")),
        check_vma=False,
    )
```

time: 492 us -> 168 us (0.34); the launches traced: 484 us -> 168 us
  waiting for transfers between devices: 314 us -> 0 us
  Pallas kernels: 0 us -> 163 us
  matrix products: 68.4 us -> 0 us
  local copies, waits for them, and re-layouts: 49.8 us -> 3.97 us
  blocking collectives: 23 us -> 0 us
  between operations: 14.3 us -> 0.66 us
  starting transfers between devices: 12.8 us -> 0 us
    unnamed x8 -> x0, waiting for transfers between devices: 314 us -> none
    pallas_call x0 -> x2, Pallas kernels: none -> 163 us  [the longest x1 90.3 us: on_device(): pl.pallas_call(compute_kernel, out_shape=(shape((3, 4, 4, 4, ROWS, 128),...]
    dot_general x11 -> x0, matrix products: 68.4 us -> none  [the longest x2 18.2 us: project_back(): lax.dot_general(left, right, (((1,), (1,)), ((), ())), precision=HIGH, pr...]
    all_to_all x1 -> x0, blocking collectives: 23 us -> none  [on_device(): lax.all_to_all(gi, 'seq', split_axis=1, concat_axis=2, tiled=True)]
    unnamed x29 -> x5, local copies, waits for them, and re-layouts: 26.6 us -> 3.97 us
    all_to_all x2 -> x0, starting transfers between devices: 12.6 us -> none  [the longest x1 6.91 us: on_device(): lax.all_to_all(x_saved, 'seq', split_axis=2, concat_axis=1, tiled=True)]
    another operation x2 -> x0, local copies, waits for them, and re-layouts: 10.3 us -> none
    reshape x2 -> x0, local copies, waits for them, and re-layouts: 7.95 us -> none  [the longest x1 5.6 us: on_device(): gqkv = jnp.stack([gq, gk, gv], axis=2).reshape(-1, 3 * width)]
  transfers between devices with their start and end apart: 6 -> 0, of which waited for: 4 -> 0; matrix products, arithmetic and copies ran while one was open for 23% -> 0% of each run, Pallas kernels for 0% -> 0%
where the time goes in v2:
time: 168 us
  Pallas kernels  163 us (97%)
  local copies, waits for them, and re-layouts  3.97 us (2%)
    pallas_call x1, Pallas kernels, on_device(): pl.pallas_call(compute_kernel, out_shape=(shape((3, 4, 4, 4, ROWS, 128),...  90.3 us
    pallas_call x1, Pallas kernels, on_device(): pl.pallas_call(exchange_kernel, out_shape=(shape((8, 4, 8, D), F32), shap...  72.8 us
    unnamed x5, local copies, waits for them, and re-layouts  3.97 us

profile of v2, /device:TPU:1, one launch (start us, length us, event | category | flops | bytes accessed | tf_op | source)
XLA Modules:
  0.0 167.7 jit_solution(18025941257358751548)
XLA Ops:
  0.6 90.3 %shard_map.76 = (f32[3,4,4,4,120,128]{5,4,3,2,1,0:T(8,128)}, f32[4,16,8,1152]{3,2,1,0:T(8,128)}) custom-call(f32[8,4,8,1152]{3,2,1,0:T(8,128)} %bitcast.5, f32[8,4,8,1152]{3,2,1,0:T(8,128)} %bitcast.6, s32[1,256]{1,0:T(1,128)} %bitcast.7, f32[1152,3456]{1,0:T(8,128)} %wqkv_hbm.1, f32[1152,1152]{1,0:T(8,128)} %wout_hbm.1), custom_call_target="tpu_custom_call" | custom-call | flops 23000000512 | bytes 40000000 | tf_op jit(solution)/shard_map/pallas_call | solution.py:640
  91.0 0.0 copy-start
  91.0 1.7 copy-done
  92.6 72.8 %shard_map.77 = (f32[8,4,8,1152]{3,2,1,0:T(8,128)S(1)}, f32[144,216]{1,0:T(8,128)S(1)}, f32[144,72]{1,0:T(8,128)S(1)}) custom-call(f32[3,4,4,4,120,128]{5,4,3,2,1,0:T(8,128)} %get-tuple-element.8.gw_hbm, f32[4,16,8,1152]{3,2,1,0:T(8,128)S(1)} %copy-done), custom_call_target="tpu_custom_call" | custom-call | flops 10000000 | bytes 40000000 | tf_op jit(solution)/shard_map/pallas_call | solution.py:687
  165.4 1.0 copy.11
  166.4 0.7 copy.12
  167.1 0.6 copy.13
Async XLA Ops:
  91.0 1.7 copy-start

commit v3 on v1

v3 whole, which is shorter than its diff:
```python
import jax
import jax.numpy as jnp
from jax import lax
from jax.experimental import pallas as pl
from jax.experimental.pallas import tpu as pltpu
from jax.sharding import PartitionSpec as P

HEADS = 16
HEAD_DIM = 72
KEEP_RATE = 0.9
D = 1152
LOCAL = 8
PART = 640
PARTS = ((24, 24, 24), (40, 40, 48), (48, 48, 64))
TOPS = (0, 72, 200)
SHARE = 360
CUTS = ((0, 64), (64, 80))
ORDERS = ((0, 1, 2), (1, 2, 0), (2, 0, 1))
MESH = pl.DeviceIdType.MESH
F32 = jnp.float32
BF16 = jnp.bfloat16

NN = (((1,), (0,)), ((), ()))
NT = (((1,), (1,)), ((), ()))


def split(value):
    high = value.astype(BF16)
    return high, (value - high.astype(F32)).astype(BF16)


def dot(left, right, dims):
    return lax.dot_general(left, right, dims, preferred_element_type=F32)


def dot3(left_high, left_low, right_high, right_low, dims):
    return (
        dot(left_high, right_high, dims)
        + dot(left_low, right_high, dims)
        + dot(left_high, right_low, dims)
    )


def iota(shape, dim):
    return lax.broadcasted_iota(jnp.int32, shape, dim)


def wait_copy(ref, sem):
    pltpu.make_async_copy(ref, ref, sem).wait()


class Share:
    def __init__(self, index, part, t, rows, here, at, gw, load, scratch, sems, last):
        self.index, self.t, self.rows = index, t, rows
        self.here, self.at = here, at
        self.gw, self.load = gw, load
        one1, two1, own1, one2, two2, own2, one3, two3 = scratch
        self.ones, self.twos = (one1, one2, one3), (two1, two2, two3)
        self.sources = (gw, own1, own2)
        self.send_sem, self.recv_sem, self.load_sem = sems
        top = TOPS[part] + sum(PARTS[part][:t])
        self.last = last.at[pl.ds(top, rows)]
        low = (rows // 16) * 8
        self.halves = (((0, 2), (2, 2)), ((0, 2), (2, 2)), ((0, rows - low), (rows - low, low)))

    def along(self, stage, step):
        axis = ORDERS[self.t][stage]
        place = list(self.here)
        place[axis] = (place[axis] + step + 4) % 4
        return self.at(*place)

    def spots(self, stage):
        me = self.here[ORDERS[self.t][stage]]
        return me, (me + 1) % 4, (me + 3) % 4, (me + 2) % 4

    def source(self, stage, spot, half):
        start, size = self.halves[stage][half]
        return self.sources[stage].at[spot, pl.ds(start, size)]

    def first_hop(self, stage, half):
        far = self.spots(stage)[3]
        size = self.halves[stage][half][1]
        return pltpu.make_async_remote_copy(
            src_ref=self.source(stage, far, half),
            dst_ref=self.ones[stage].at[half, pl.ds(0, size)],
            send_sem=self.send_sem.at[self.index, stage, half],
            recv_sem=self.recv_sem.at[self.index, stage, half],
            device_id=self.along(stage, 1 if half == 0 else -1),
            device_id_type=MESH,
        )

    def second_hop(self, stage, way, half):
        me, up, down, far = self.spots(stage)
        start, size = self.halves[stage][half]
        if half == way:
            src = self.ones[stage].at[half, pl.ds(0, size)]
        else:
            src = self.source(stage, up if way == 0 else down, half)
        slot = 2 + 2 * way + half
        return pltpu.make_async_remote_copy(
            src_ref=src,
            dst_ref=self.twos[stage].at[way, pl.ds(start, size)],
            send_sem=self.send_sem.at[self.index, stage, slot],
            recv_sem=self.recv_sem.at[self.index, stage, slot],
            device_id=self.along(stage, 1 if way == 0 else -1),
            device_id_type=MESH,
        )

    def loads(self):
        me, up, down, far = self.spots(0)
        copy = pltpu.make_async_copy
        return (
            copy(self.source(0, up, 0), self.load.at[0], self.load_sem.at[self.index, 0]),
            copy(self.source(0, down, 1), self.load.at[1], self.load_sem.at[self.index, 1]),
            copy(self.gw.at[me], self.sources[1], self.load_sem.at[self.index, 2]),
        )

    def middle(self, stage):
        me, up, down, far = self.spots(stage)
        for way in range(2):
            self.first_hop(stage, way).wait_recv()
            size = self.halves[stage][way][1]
            to = self.ones[stage].at[way, pl.ds(0, size)]
            if stage == 0:
                to[...] = to[...] + self.load[way]
            else:
                to[...] = to[...] + self.source(stage, up if way == 0 else down, way)[...]
            self.second_hop(stage, way, way).start()

    def close(self, stage):
        me = self.spots(stage)[0]
        for way in range(2):
            for half in range(2):
                self.second_hop(stage, way, half).wait_recv()
        two = self.twos[stage]
        if stage == 0:
            own = self.sources[1]
            own[...] = own[...] + two[0] + two[1]
        elif stage == 1:
            own = self.sources[2]
            own[...] = self.sources[1][me] + two[0] + two[1]
        else:
            self.last[...] = self.sources[2][me] + two[0] + two[1]

    def finish(self):
        for stage in range(3):
            for half in range(2):
                self.first_hop(stage, half).wait_send()
                for way in range(2):
                    self.second_hop(stage, way, half).wait_send()


def open_stage(shares, stage):
    for half in range(2):
        for share in shares:
            share.first_hop(stage, half).start()
    for way in range(2):
        for share in shares:
            share.second_hop(stage, way, 1 - way).start()


def middle(shares, stage):
    for share in shares:
        share.middle(stage)


def close(shares, stage):
    for share in shares:
        share.close(stage)


def scratch_of(rows):
    vmem = pltpu.VMEM
    return [
        vmem((2, 2, 4, rows, 128), F32),
        vmem((2, 4, 4, rows, 128), F32),
        vmem((4, 4, rows, 128), F32),
        vmem((2, 2, rows, 128), F32),
        vmem((2, 4, rows, 128), F32),
        vmem((4, rows, 128), F32),
        vmem((2, rows - (rows // 16) * 8, 128), F32),
        vmem((2, rows, 128), F32),
    ]


def stack(high, low):
    return jnp.concatenate([high, low], axis=0)


def all_nt(left, right):
    rows = left.shape[0] // 2
    columns = right.shape[0] // 2
    full = dot(left, right, NT)
    return (full[:rows, :columns] + full[:rows, columns:]) + (full[rows:, :columns] + full[rows:, columns:])


def all_nn(left, right):
    rows = left.shape[0] // 2
    full = dot(jnp.concatenate([left, left], axis=1), right, NN)
    return full[:rows] + full[rows:]


def kernel(*refs):
    x_hbm, g_hbm, mask_ref, wqkv_hbm, wout_hbm = refs[0:5]
    input_out, qkv_out, out_out = refs[5:8]
    gw = [refs[8 + 3 * part : 11 + 3 * part] for part in range(3)]
    (
        xl, gl, gsrc, sel, wph, wpl, woh, wol, xth1, xtl1, xth2, xtl2, qkv, gqkv, gm, mixed, probs, mth, mtl,
        gph, gpl, big_h, big_l, gqh, gql, outw, last, other,
        xs_sem, xr_sem, xfs_sem, xfr_sem, gs_sem, gr_sem, gfs_sem, gfr_sem, loc_sem, w_sem, gw_sem, out_sem,
        rs_send, rs_recv, ld_sem, gx_send, gx_recv, ga_send, ga_recv, fin_sem,
    ) = refs[17:65]
    rest = refs[65:]
    stage_refs = [rest[0:3], rest[3:6]]
    load_refs = rest[6:9]
    rest = rest[9:]

    clip = lax.axis_index("clip")
    seq = lax.axis_index("seq")
    chip = seq // 2
    core = seq % 2
    sibling = (clip, 2 * chip + 1 - core)
    here = (2 * (clip % 2) + chip % 2, chip // 2, clip // 2)

    def at(x, y, z):
        return (2 * z + x // 2, 4 * y + 2 * (x % 2) + core)

    shares = []
    for part in range(3):
        for t in range(3):
            index = 3 * part + t
            rows = PARTS[part][t]
            load = load_refs[t].at[:, :, :, pl.ds(0, rows)]
            shares.append(
                Share(index, part, t, rows, here, at, gw[part][t], load,
                      rest[8 * index : 8 * index + 8], (rs_send, rs_recv, ld_sem), last)
            )
    out_shares, first_shares, second_shares = shares[0:3], shares[3:6], shares[6:9]

    def peer(d):
        return (clip, 2 * ((chip + d) % 8) + core)

    def frame_from(d, c):
        return 2 * ((chip + 8 - d) % 8) + c

    barrier = pltpu.get_barrier_semaphore()
    for d in range(1, 8):
        pl.semaphore_signal(barrier, inc=1, device_id=peer(d), device_id_type=MESH)
    pl.semaphore_signal(barrier, inc=1, device_id=sibling, device_id_type=MESH)
    for t in range(3):
        for step in (1, -1):
            pl.semaphore_signal(
                barrier, inc=1, device_id=out_shares[t].along(0, step), device_id_type=MESH
            )

    own_frame = 2 * chip + core
    load_x = pltpu.make_async_copy(x_hbm.at[chip], xl.at[:, own_frame], loc_sem.at[0])
    load_x.start()
    load_g = pltpu.make_async_copy(g_hbm, gsrc, loc_sem.at[1])
    load_g.start()

    def weight_copy(step, slot):
        rows = pl.ds(pl.multiple_of((step % 6) * 192, 8), 192)
        columns = pl.ds(pl.multiple_of((step // 6) * D, 128), D)
        to = pl.ds(pl.multiple_of(slot * 192, 8), 192)
        return pltpu.make_async_copy(wqkv_hbm.at[rows, columns], qkv.at[to, pl.ds(0, D)], w_sem.at[slot])

    weight_copy(0, 0).start()
    pl.semaphore_wait(barrier, 14)

    def send(src, dst, send_sems, recv_sems, d):
        p = (chip + d) % 8
        return pltpu.make_async_remote_copy(
            src_ref=src.at[p],
            dst_ref=dst.at[:, own_frame],
            send_sem=send_sems.at[d],
            recv_sem=recv_sems.at[d],
            device_id=peer(d),
            device_id_type=MESH,
        )

    def same_place(view, send_sems, recv_sems, d, device):
        return pltpu.make_async_remote_copy(
            src_ref=view, dst_ref=view, send_sem=send_sems.at[d], recv_sem=recv_sems.at[d],
            device_id=device, device_id_type=MESH,
        )

    def arrival(dst, send_sems, recv_sems, d):
        return same_place(dst.at[:, frame_from(d, core)], send_sems, recv_sems, d, peer(d))

    def forward(dst, send_sems, recv_sems, d):
        return same_place(dst.at[:, frame_from(d, core)], send_sems, recv_sems, d, sibling)

    def forwarded(dst, send_sems, recv_sems, d):
        return same_place(dst.at[:, frame_from(d, 1 - core)], send_sems, recv_sems, d, sibling)

    for d in range(1, 8):
        send(x_hbm, xl, xs_sem, xr_sem, d).start()

    load_g.wait()
    same = iota((256, 256), 0) == iota((256, 256), 1)
    keep = mask_ref[...].astype(F32)
    column = jnp.sum(jnp.where(same, keep, 0.0), axis=1, keepdims=True) / KEEP_RATE
    column = column.reshape(8, 4, 8, 1)
    for p in range(8):
        gsrc[p] = gsrc[p] * column[p]

    bases = (0, 128, 384, 640, 640)
    for n in range(5):
        lane = iota((512, 128), 1) + 128 * n
        head = lane // HEAD_DIM
        source = lane + HEAD_DIM * (head + core) - bases[n]
        hit = (iota((512, 128), 0) == source) & (lane < LOCAL * HEAD_DIM)
        sel[n] = jnp.where(hit, 1.0, 0.0).astype(BF16)

    load_x.wait()
    forward(xl, xfs_sem, xfr_sem, 0).start()

    def head_copy(a):
        return pltpu.make_async_copy(
            wout_hbm.at[pl.ds(HEAD_DIM * (2 * a + core), HEAD_DIM)],
            outw.at[a // 2, a % 2],
            w_sem.at[2 + a],
        )

    for a in range(LOCAL):
        head_copy(a).start()

    def prepare(step, carry):
        slot = step % 2

        @pl.when(step < 17)
        def _():
            weight_copy(step + 1, 1 - slot).start()

        weight_copy(step, slot).wait()
        rows = pl.ds(pl.multiple_of((step % 6) * 192, 16), 192)
        staged = pl.ds(pl.multiple_of(slot * 192, 8), 192)
        part = step // 6
        for n in range(5):
            high, low = split(qkv[staged, bases[n] : bases[n] + 512])
            to = pl.ds(pl.multiple_of(PART * part + 128 * n, 128), 128)
            wph[rows, to] = dot(high, sel[n], NN).astype(BF16)
            wpl[rows, to] = dot(low, sel[n], NN).astype(BF16)
        return carry

    lax.fori_loop(0, 18, prepare, 0)

    own_g = pltpu.make_async_copy(gsrc.at[chip], gl.at[:, own_frame], loc_sem.at[2])
    own_g.start()
    for d in range(1, 8):
        send(x_hbm, xl, xs_sem, xr_sem, d).wait_send()
        send(gsrc, gl, gs_sem, gr_sem, d).start()
    for d in range(1, 8):
        arrival(xl, xs_sem, xr_sem, d).wait_recv()
        forward(xl, xfs_sem, xfr_sem, d).start()

    for a in range(LOCAL):
        head_copy(a).wait()
    for n in range(4):
        high, low = split(outw[n].reshape(144, D))
        woh[144 * n : 144 * n + 144, :] = high
        wol[144 * n : 144 * n + 144, :] = low
    woh[576:640, :] = jnp.zeros((64, D), BF16)
    wol[576:640, :] = jnp.zeros((64, D), BF16)
    for part in range(3):
        gqkv[:, PART * part + 512 : PART * part + 640] = jnp.zeros((128, 128), F32)
    mixed[:, 512:640] = jnp.zeros((128, 128), F32)

    for d in range(8):
        forwarded(xl, xfs_sem, xfr_sem, d).wait_recv()
    own_g.wait()
    forward(gl, gfs_sem, gfr_sem, 0).start()

    def split_x(g, carry):
        rows = pl.ds(pl.multiple_of(g * 128, 128), 128)
        value = xl[g].reshape(128, D)
        high, low = split(value)
        big_h[rows, 0:D] = high
        big_l[rows, 0:D] = low
        high, low = split(value.T)
        for i in range(8):
            xth1[64 * i : 64 * i + 64, rows] = high[144 * i : 144 * i + 64]
            xtl1[64 * i : 64 * i + 64, rows] = low[144 * i : 144 * i + 64]
            xth2[80 * i : 80 * i + 80, rows] = high[144 * i + 64 : 144 * i + 144]
            xtl2[80 * i : 80 * i + 80, rows] = low[144 * i + 64 : 144 * i + 144]
        return carry

    lax.fori_loop(0, 4, split_x, 0)

    def project(first, width):
        to = pl.ds(first, width)
        qkv[:, to] = dot3(
            big_h[:, 0:D], big_l[:, 0:D], wph[:, to], wpl[:, to], NN
        )

    def project_tile(n, carry):
        project(pl.multiple_of(n * 256, 256), 256)
        return carry

    lax.fori_loop(0, 7, project_tile, 0)
    project(1792, 128)
    for d in range(8):
        forward(xl, xfs_sem, xfr_sem, d).wait_send()
    for d in range(1, 8):
        arrival(gl, gs_sem, gr_sem, d).wait_recv()
        forward(gl, gfs_sem, gfr_sem, d).start()

    scaling = HEAD_DIM ** (-0.5)
    firsts = [min(HEAD_DIM * a // 128 * 128, 384) for a in range(LOCAL)]

    def own_lanes(a):
        lane = iota((128, 256), 1)
        low_lane = HEAD_DIM * a - firsts[a]
        return (lane >= low_lane) & (lane < low_lane + HEAD_DIM)

    def window(ref, rows, part, a):
        start = PART * part + firsts[a]
        return ref[rows, start : start + 256]

    def attend(g, carry):
        rows = pl.ds(pl.multiple_of(g * 128, 128), 128)
        same_patch = (iota((128, 128), 0) % 8) == (iota((128, 128), 1) % 8)
        for a in range(LOCAL):
            mine = own_lanes(a)
            q = stack(*split(jnp.where(mine, window(qkv, rows, 0, a), 0.0) * scaling))
            k = stack(*split(window(qkv, rows, 1, a)))
            v = stack(*split(window(qkv, rows, 2, a)))
            scores = jnp.where(same_patch, all_nt(q, k), -1e30)
            expo = jnp.exp(scores - jnp.max(scores, axis=1, keepdims=True))
            attn = expo / jnp.sum(expo, axis=1, keepdims=True)
            probs[g, a] = attn
            pltpu.store(
                mixed.at[:, firsts[a] : firsts[a] + 256], all_nn(stack(*split(attn)), v), mask=mine
            )
        high, low = split(mixed[...].T)
        mth[:, rows] = high
        mtl[:, rows] = low
        return carry

    lax.fori_loop(0, 4, attend, 0)

    for d in range(8):
        forwarded(gl, gfs_sem, gfr_sem, d).wait_recv()

    def regroup(g, carry):
        rows = pl.ds(pl.multiple_of(g * 128, 128), 128)
        value = gl[g].reshape(128, D)
        high, low = split(value)
        gqh[rows, 0:D] = high
        gql[rows, 0:D] = low
        lane = iota((128, 128), 1)
        rest = value[:, 128:256]
        for j in range(8):
            tile = 144 * j // 128
            offset = 144 * j % 128
            if offset:
                piece = value[:, 128 * tile : 128 * tile + 256]
                piece = pltpu.roll(piece, 256 - offset, 1)[:, 0:128]
            else:
                piece = value[:, 128 * tile : 128 * tile + 128]
            high, low = split(piece)
            gph[rows, 128 * j : 128 * j + 128] = high
            gpl[rows, 128 * j : 128 * j + 128] = low
            if j:
                rest = jnp.where(lane // 16 == j, value[:, 128 * (j + 1) : 128 * (j + 2)], rest)
        high, low = split(rest)
        gph[rows, 1024:1152] = high
        gpl[rows, 1024:1152] = low
        return carry

    lax.fori_loop(0, 4, regroup, 0)

    def out_tile(first, width):
        to = pl.ds(first, width)
        term = dot3(mth[...], mtl[...], gph[:, to], gpl[:, to], NN)
        outw[:, :, :, to] = term[0:576].reshape(4, 2, 72, width)

    def out_step(n, carry):
        out_tile(pl.multiple_of(n * 256, 256), 256)
        return carry

    lax.fori_loop(0, 4, out_step, 0)
    out_tile(1024, 128)

    def targets(part, dx, dy):
        first, second, third = gw[part]
        return (first.at[dx, dy], second.at[dy, :, dx], third.at[:, dx, dy])

    def out_copies(j):
        columns = pl.ds(pl.multiple_of(j * 128, 128), 128)
        copies = []
        for dx_high in range(2):
            for t, target in enumerate(targets(0, 2 * dx_high + j % 2, j // 2)):
                copies.append(
                    pltpu.make_async_copy(
                        outw.at[:, dx_high, pl.ds(24 * t, 24), columns], target, out_sem.at[j, 3 * dx_high + t]
                    )
                )
        return copies

    def out_start(j, carry):
        for copy in out_copies(j):
            copy.start()
        return carry

    def out_wait(j, carry):
        for copy in out_copies(j):
            copy.wait()
        return carry

    lax.fori_loop(0, 8, out_start, 0)

    for first, width in ((0, 256), (256, 256), (512, 128)):
        gm[:, first : first + width] = dot3(
            gqh[:, 0:D], gql[:, 0:D], woh[first : first + width, :], wol[first : first + width, :], NT
        )

    lax.fori_loop(0, 8, out_wait, 0)
    open_stage(out_shares, 0)
    for share in out_shares:
        for copy in share.loads():
            copy.start()
    for share in out_shares:
        for copy in share.loads():
            copy.wait()

    def attend_back(g, carry):
        rows = pl.ds(pl.multiple_of(g * 128, 128), 128)

        def put(part, a, value):
            start = PART * part + firsts[a]
            pltpu.store(gqkv.at[:, start : start + 256], value, mask=own_lanes(a))

        for a in range(LOCAL):
            mine = own_lanes(a)
            q = stack(*split(jnp.where(mine, window(qkv, rows, 0, a), 0.0) * scaling))
            k = stack(*split(window(qkv, rows, 1, a)))
            v = stack(*split(window(qkv, rows, 2, a)))
            m = stack(*split(jnp.where(mine, gm[rows, firsts[a] : firsts[a] + 256], 0.0)))
            attn = probs[g, a]
            grad_attn = all_nt(m, v)
            grad_scores = attn * (grad_attn - jnp.sum(grad_attn * attn, axis=1, keepdims=True))
            put(0, a, all_nn(stack(*split(grad_scores)), k) * scaling)
            put(1, a, all_nn(stack(*split(grad_scores.T)), q))
            put(2, a, all_nn(stack(*split(attn.T)), m))

        high, low = split(gqkv[...])
        gqh[rows, :] = high
        gql[rows, :] = low
        lane = iota((128, 256), 1)
        for j in range(8):
            starts = [PART * ((3 * j + k) // 8) + HEAD_DIM * ((3 * j + k) % 8) for k in range(3)]
            base = starts[0] // 128 * 128
            end = -(-(starts[2] + HEAD_DIM) // 128) * 128
            span = gqkv[:, base:end]
            value = jnp.zeros((128, 256), F32)
            done = {}
            for k in range(3):
                shift = (starts[k] - base - HEAD_DIM * k) % (end - base)
                if shift not in done:
                    moved = span if shift == 0 else pltpu.roll(span, end - base - shift, 1)
                    done[shift] = moved[:, 0:256]
                value = jnp.where((lane >= HEAD_DIM * k) & (lane < HEAD_DIM * k + HEAD_DIM), done[shift], value)
            high, low = split(value)
            big_h[rows, 256 * j : 256 * j + 256] = high
            big_l[rows, 256 * j : 256 * j + 256] = low
        return carry

    lax.fori_loop(0, 2, attend_back, 0)
    middle(out_shares, 0)
    lax.fori_loop(2, 4, attend_back, 0)
    close(out_shares, 0)
    open_stage(out_shares, 1)

    def gw_copies(which, j, slot):
        copies = []
        for dx_high in range(2):
            for t, target in enumerate(targets(1 + which, 2 * dx_high + j % 2, j // 2)):
                copies.append(
                    pltpu.make_async_copy(
                        stage_refs[which][t].at[slot, dx_high], target, gw_sem.at[which, slot, 3 * dx_high + t]
                    )
                )
        return copies

    def gw_part(which):
        high_ref, low_ref = ((xth1, xtl1), (xth2, xtl2))[which]
        size = CUTS[which][1]

        def gw_step(j, carry):
            slot = j % 2

            @pl.when(j >= 2)
            def _():
                for copy in gw_copies(which, j - 2, slot):
                    copy.wait()

            to = pl.ds(pl.multiple_of(j * 256, 256), 256)
            term = dot3(high_ref[...], low_ref[...], big_h[:, to], big_l[:, to], NN)
            inside = iota((8, 128), 1)
            inside = (inside >= 88) & (inside < 104)
            for i in range(8):
                dz, dx_high = i // 2, i % 2
                if which == 1:
                    rest = pltpu.roll(outw[dz, dx_high, :, 1024:1152], (88 + 128 - 16 * j) % 128, 1)
                top = 0
                for t in range(3):
                    for r in range(0, PARTS[1 + which][t], 8):
                        row = top + r
                        if row < size:
                            value = term[size * i + row : size * i + row + 8, 0:128]
                        else:
                            row = row - size
                            value = term[size * i + row : size * i + row + 8, 128:256]
                            if which == 1 and row < HEAD_DIM:
                                value = jnp.where(inside, rest[row : row + 8], value)
                        stage_refs[which][t][slot, dx_high, dz, r : r + 8, :] = value
                    top += PARTS[1 + which][t]
            for copy in gw_copies(which, j, slot):
                copy.start()
            return carry

        lax.fori_loop(0, 8, gw_step, 0)
        for j in (6, 7):
            for copy in gw_copies(which, j, j % 2):
                copy.wait()

    gw_part(0)
    open_stage(first_shares, 0)
    for share in first_shares:
        for copy in share.loads():
            copy.start()
    middle(out_shares, 1)
    close(out_shares, 1)
    open_stage(out_shares, 2)
    gw_part(1)
    for share in first_shares:
        for copy in share.loads():
            copy.wait()
    middle(first_shares, 0)
    open_stage(second_shares, 0)
    for share in second_shares:
        for copy in share.loads():
            copy.start()
    middle(out_shares, 2)
    close(out_shares, 2)

    def gi_cross(p):
        return pltpu.make_async_remote_copy(
            src_ref=gl.at[:, 2 * p + 1 - core],
            dst_ref=xl.at[:, 2 * p + 1 - core],
            send_sem=gx_send.at[p],
            recv_sem=gx_recv.at[p],
            device_id=sibling,
            device_id_type=MESH,
        )

    def gi_crossed(p):
        return same_place(xl.at[:, 2 * p + core], gx_send, gx_recv, p, sibling)

    def gi_back(d):
        return pltpu.make_async_remote_copy(
            src_ref=gl.at[:, 2 * ((chip + d) % 8) + core],
            dst_ref=input_out.at[chip],
            send_sem=ga_send.at[d],
            recv_sem=ga_recv.at[d],
            device_id=peer(d),
            device_id_type=MESH,
        )

    def gi_arrival(d):
        return same_place(input_out.at[(chip + 8 - d) % 8], ga_send, ga_recv, d, peer(d))

    for d in range(1, 8):
        send(gsrc, gl, gs_sem, gr_sem, d).wait_send()
    for d in range(8):
        forward(gl, gfs_sem, gfr_sem, d).wait_send()

    def input_tile(first, width):
        to = pl.ds(first, width)
        term = dot3(gqh[...], gql[...], wph[to, :], wpl[to, :], NT)
        gl[:, :, :, to] = term.reshape(4, 16, 8, width)

    def input_step(n, carry):
        input_tile(pl.multiple_of(n * 256, 256), 256)
        return carry

    lax.fori_loop(0, 4, input_step, 0)
    input_tile(1024, 128)
    for p in range(8):
        gi_cross(p).start()
    close(first_shares, 0)
    open_stage(first_shares, 1)
    for share in second_shares:
        for copy in share.loads():
            copy.wait()
    middle(second_shares, 0)
    for d in range(8):
        p = (chip + d) % 8
        gi_crossed(p).wait_recv()
        mine = 2 * p + core
        gl[:, mine] = gl[:, mine] + xl[:, mine]
        if d:
            gi_back(d).start()
    own_input = pltpu.make_async_copy(gl.at[:, own_frame], input_out.at[chip], fin_sem.at[0])
    own_input.start()
    middle(first_shares, 1)
    close(second_shares, 0)
    open_stage(second_shares, 1)
    close(first_shares, 1)
    open_stage(first_shares, 2)
    middle(second_shares, 1)
    middle(first_shares, 2)
    close(second_shares, 1)
    open_stage(second_shares, 2)
    close(first_shares, 2)

    def swap(start, size, sem):
        return pltpu.make_async_remote_copy(
            src_ref=last.at[pl.ds(start, size)], dst_ref=other.at[pl.ds(start, size)],
            send_sem=fin_sem.at[sem], recv_sem=fin_sem.at[sem + 1],
            device_id=sibling, device_id_type=MESH,
        )

    swaps = (swap(0, TOPS[2], 1), swap(TOPS[2], SHARE - TOPS[2], 3))
    swaps[0].start()
    middle(second_shares, 2)
    close(second_shares, 2)
    swaps[1].start()
    swaps[0].wait_recv()

    even = core == 0

    def qkv_rows(which):
        first, size = CUTS[which]
        top = TOPS[1 + which]

        def both(ref):
            return jnp.concatenate([ref[top : top + size], ref[top + size : top + 2 * size]], axis=1)

        def turn(value):
            return jnp.where(even, pltpu.roll(value, HEAD_DIM, 1), pltpu.roll(value, 256 - HEAD_DIM, 1))

        mine, yours = both(last), both(other)
        lane = iota((size, 256), 1)
        turned = turn(mine)
        left = jnp.where(even, mine, turned)
        right = jnp.where(even, turned, mine)
        whole = jnp.where(lane < HEAD_DIM, left, jnp.where(lane < 2 * HEAD_DIM, turn(yours), right))
        qkv_out[first : first + size, :] = whole[:, 0:216]

    qkv_rows(0)
    swaps[1].wait_recv()
    qkv_rows(1)

    def out_rows(ref):
        lane = iota((72, 128), 1)
        main = ref[0:72]
        rest = pltpu.roll(ref[TOPS[2] + 80 : TOPS[2] + 152], 128 - 32, 1)
        return jnp.where(even, main, jnp.where(lane < 56, pltpu.roll(main, 128 - HEAD_DIM, 1), rest))

    a = out_rows(last)
    b = out_rows(other)
    out_out[0:72, :] = jnp.where(even, a, b)[:, 0:HEAD_DIM]
    out_out[72:144, :] = jnp.where(even, b, a)[:, 0:HEAD_DIM]

    for d in range(1, 8):
        gi_arrival(d).wait_recv()
        gi_back(d).wait_send()
    for p in range(8):
        gi_cross(p).wait_send()
    for share in shares:
        share.finish()
    for copy in swaps:
        copy.wait_send()
    own_input.wait()


def on_device(x_saved, grad_out, keep_mask, w_qkv, w_out):
    any_space = pl.BlockSpec(memory_space=pl.ANY)
    in_vmem = pl.BlockSpec(memory_space=pltpu.VMEM)
    dma = pltpu.SemaphoreType.DMA
    shape = jax.ShapeDtypeStruct
    vmem = pltpu.VMEM
    heaps = [shape((4, 4, 4, rows, 128), F32) for part in PARTS for rows in part]
    scratch = [
        vmem((4, 16, 8, D), F32),
        vmem((4, 16, 8, D), F32),
        vmem((8, 4, 8, D), F32),
        vmem((5, 512, 128), BF16),
        vmem((D, 3 * PART), BF16),
        vmem((D, 3 * PART), BF16),
        vmem((PART, D), BF16),
        vmem((PART, D), BF16),
        vmem((512, 512), BF16),
        vmem((512, 512), BF16),
        vmem((640, 512), BF16),
        vmem((640, 512), BF16),
        vmem((512, 3 * PART), F32),
        vmem((128, 3 * PART), F32),
        vmem((512, PART), F32),
        vmem((128, PART), F32),
        vmem((4, LOCAL, 128, 128), F32),
        vmem((PART, 512), BF16),
        vmem((PART, 512), BF16),
        vmem((512, D), BF16),
        vmem((512, D), BF16),
        vmem((512, 2048), BF16),
        vmem((512, 2048), BF16),
        vmem((512, 3 * PART), BF16),
        vmem((512, 3 * PART), BF16),
        vmem((4, 2, 72, D), F32),
        vmem((SHARE, 128), F32),
        vmem((SHARE, 128), F32),
        dma((8,)), dma((8,)), dma((8,)), dma((8,)),
        dma((8,)), dma((8,)), dma((8,)), dma((8,)),
        dma((3,)), dma((10,)), dma((2, 2, 6)), dma((8, 6)),
        dma((9, 3, 6)), dma((9, 3, 6)), dma((9, 3)),
        dma((8,)), dma((8,)), dma((8,)), dma((8,)), dma((5,)),
    ]
    for part in (1, 2):
        scratch += [vmem((2, 2, 4, rows, 128), F32) for rows in PARTS[part]]
    scratch += [vmem((2, 2, 4, max(part[t] for part in PARTS), 128), F32) for t in range(3)]
    for part in PARTS:
        for rows in part:
            scratch += scratch_of(rows)
    outputs = pl.pallas_call(
        kernel,
        out_shape=[shape((8, 4, 8, D), F32), shape((144, 216), F32), shape((144, 72), F32)] + heaps,
        in_specs=[any_space, any_space, in_vmem, any_space, any_space],
        out_specs=[any_space, in_vmem, in_vmem] + [any_space] * 9,
        scratch_shapes=scratch,
        compiler_params=pltpu.CompilerParams(
            collective_id=0, has_side_effects=True, vmem_limit_bytes=64 * 2**20
        ),
        cost_estimate=pl.CostEstimate(flops=23 * 10**9, bytes_accessed=60 * 10**6, transcendentals=10**6),
    )(
        x_saved.reshape(8, 4, 8, D),
        grad_out.reshape(8, 4, 8, D),
        keep_mask.reshape(1, 256),
        w_qkv,
        w_out,
    )
    return (outputs[0].reshape(1, 1, 256, D), outputs[1], outputs[2])


def solution(mesh):
    return jax.shard_map(
        on_device,
        mesh=mesh,
        in_specs=(
            P("clip", "seq", None, None),
            P("clip", "seq", None, None),
            P("clip", "seq", None),
            P(),
            P(),
        ),
        out_specs=(P("clip", "seq", None, None), P("clip", "seq"), P("clip", "seq")),
        check_vma=False,
    )
```

time: 492 us -> 171 us (0.35); the launches traced: 484 us -> 171 us
  waiting for transfers between devices: 314 us -> 0 us
  Pallas kernels: 0 us -> 167 us
  matrix products: 68.4 us -> 0 us
  local copies, waits for them, and re-layouts: 49.8 us -> 3.7 us
  blocking collectives: 23 us -> 0 us
  between operations: 14.3 us -> 0.66 us
  starting transfers between devices: 12.8 us -> 0 us
    unnamed x8 -> x0, waiting for transfers between devices: 314 us -> none
    pallas_call x0 -> x1, Pallas kernels: none -> 167 us  [on_device(): pl.pallas_call(kernel, out_shape=[shape((8, 4, 8, D), F32), shape((144, 2...]
    dot_general x11 -> x0, matrix products: 68.4 us -> none  [the longest x2 18.2 us: project_back(): lax.dot_general(left, right, (((1,), (1,)), ((), ())), precision=HIGH, pr...]
    all_to_all x1 -> x0, blocking collectives: 23 us -> none  [on_device(): lax.all_to_all(gi, 'seq', split_axis=1, concat_axis=2, tiled=True)]
    unnamed x29 -> x7, local copies, waits for them, and re-layouts: 26.6 us -> 3.7 us
    all_to_all x2 -> x0, starting transfers between devices: 12.6 us -> none  [the longest x1 6.91 us: on_device(): lax.all_to_all(x_saved, 'seq', split_axis=2, concat_axis=1, tiled=True)]
    another operation x2 -> x0, local copies, waits for them, and re-layouts: 10.3 us -> none
    reshape x2 -> x0, local copies, waits for them, and re-layouts: 7.95 us -> none  [the longest x1 5.6 us: on_device(): gqkv = jnp.stack([gq, gk, gv], axis=2).reshape(-1, 3 * width)]
  transfers between devices with their start and end apart: 6 -> 0, of which waited for: 4 -> 0; matrix products, arithmetic and copies ran while one was open for 23% -> 0% of each run, Pallas kernels for 0% -> 0%
where the time goes in v3:
time: 171 us
  Pallas kernels  167 us (98%)
  local copies, waits for them, and re-layouts  3.7 us (2%)
    pallas_call x1, Pallas kernels, on_device(): pl.pallas_call(kernel, out_shape=[shape((8, 4, 8, D), F32), shape((144, 2...  167 us
    unnamed x7, local copies, waits for them, and re-layouts  3.7 us

profile of v3, /device:TPU:1, one launch (start us, length us, event | category | flops | bytes accessed | tf_op | source)
XLA Modules:
  0.0 170.9 jit_solution(663501615801765659)
XLA Ops:
  0.6 166.6 %shard_map.76 = (f32[8,4,8,1152]{3,2,1,0:T(8,128)}, f32[144,216]{1,0:T(8,128)}, f32[144,72]{1,0:T(8,128)}, f32[4,4,4,24,128]{4,3,2,1,0:T(8,128)}, f32[4,4,4,24,1...) custom-call(f32[8,4,8,1152]{3,2,1,0:T(8,128)} %bitcast.5, ...), custom_call_target="tpu_custom_call" | custom-call | flops 23000000512 | bytes 60000000 | tf_op jit(solution)/shard_map/pallas_call | solution.py:828
  167.2 0.0 copy-start
  167.2 0.0 copy-start.1
  167.2 2.4 %copy.11 = f32[1,1,256,1152]{3,2,1,0:T(8,128)} copy(f32[1,1,256,1152]{3,2,1,0:T(8,128)} %bitcast.4) | data formatting | bytes 2359296
  169.6 0.0 copy-done
  169.7 0.7 copy.12
  170.3 0.0 copy-done.1
  170.3 0.6 copy.13
Async XLA Ops:
  167.2 2.4 %copy-start = (f32[144,216]{1,0:T(8,128)S(1)}, f32[144,216]{1,0:T(8,128)}, u32[]{:S(2)}) copy-start(f32[144,216]{1,0:T(8,128)} %get-tuple-element.13) | copy-start | bytes 373252
  167.2 3.1 %copy-start.1 = (f32[144,72]{1,0:T(8,128)S(1)}, f32[144,72]{1,0:T(8,128)}, u32[]{:S(2)}) copy-start(f32[144,72]{1,0:T(8,128)} %get-tuple-element.14) | copy-start | bytes 124420

commit v4 on v3

--- a/solution.py
+++ b/solution.py
@@ -54,14 +54,13 @@
         self.index, self.t, self.rows = index, t, rows
         self.here, self.at = here, at
         self.gw, self.load = gw, load
-        one1, two1, own1, one2, two2, own2, one3, two3 = scratch
-        self.ones, self.twos = (one1, one2, one3), (two1, two2, two3)
+        one1, two1, own1, one2, two2, own2, three = scratch
+        self.ones, self.twos, self.three = (one1, one2), (two1, two2), three
         self.sources = (gw, own1, own2)
         self.send_sem, self.recv_sem, self.load_sem = sems
         top = TOPS[part] + sum(PARTS[part][:t])
         self.last = last.at[pl.ds(top, rows)]
-        low = (rows // 16) * 8
-        self.halves = (((0, 2), (2, 2)), ((0, 2), (2, 2)), ((0, rows - low), (rows - low, low)))
+        self.halves = (((0, 2), (2, 2)), ((0, 2), (2, 2)))
 
     def along(self, stage, step):
         axis = ORDERS[self.t][stage]
@@ -106,6 +105,17 @@
             device_id_type=MESH,
         )
 
+    def direct(self, way):
+        step = (1, -1, 2)[way]
+        return pltpu.make_async_remote_copy(
+            src_ref=self.sources[2].at[(self.spots(2)[0] + step + 4) % 4],
+            dst_ref=self.three.at[way],
+            send_sem=self.send_sem.at[self.index, 2, way],
+            recv_sem=self.recv_sem.at[self.index, 2, way],
+            device_id=self.along(2, step),
+            device_id_type=MESH,
+        )
+
     def loads(self):
         me, up, down, far = self.spots(0)
         copy = pltpu.make_async_copy
@@ -129,6 +139,11 @@
 
     def close(self, stage):
         me = self.spots(stage)[0]
+        if stage == 2:
+            for way in range(3):
+                self.direct(way).wait_recv()
+            self.last[...] = self.sources[2][me] + self.three[0] + self.three[1] + self.three[2]
+            return
         for way in range(2):
             for half in range(2):
                 self.second_hop(stage, way, half).wait_recv()
@@ -136,21 +151,26 @@
         if stage == 0:
             own = self.sources[1]
             own[...] = own[...] + two[0] + two[1]
-        elif stage == 1:
+        else:
             own = self.sources[2]
             own[...] = self.sources[1][me] + two[0] + two[1]
-        else:
-            self.last[...] = self.sources[2][me] + two[0] + two[1]
 
     def finish(self):
-        for stage in range(3):
+        for stage in range(2):
             for half in range(2):
                 self.first_hop(stage, half).wait_send()
                 for way in range(2):
                     self.second_hop(stage, way, half).wait_send()
+        for way in range(3):
+            self.direct(way).wait_send()
 
 
 def open_stage(shares, stage):
+    if stage == 2:
+        for way in (2, 0, 1):
+            for share in shares:
+                share.direct(way).start()
+        return
     for half in range(2):
         for share in shares:
             share.first_hop(stage, half).start()
@@ -178,8 +198,7 @@
         vmem((2, 2, rows, 128), F32),
         vmem((2, 4, rows, 128), F32),
         vmem((4, rows, 128), F32),
-        vmem((2, rows - (rows // 16) * 8, 128), F32),
-        vmem((2, rows, 128), F32),
+        vmem((3, rows, 128), F32),
     ]
 
 
@@ -233,7 +252,7 @@
             load = load_refs[t].at[:, :, :, pl.ds(0, rows)]
             shares.append(
                 Share(index, part, t, rows, here, at, gw[part][t], load,
-                      rest[8 * index : 8 * index + 8], (rs_send, rs_recv, ld_sem), last)
+                      rest[7 * index : 7 * index + 7], (rs_send, rs_recv, ld_sem), last)
             )
     out_shares, first_shares, second_shares = shares[0:3], shares[3:6], shares[6:9]
 
@@ -248,7 +267,7 @@
         pl.semaphore_signal(barrier, inc=1, device_id=peer(d), device_id_type=MESH)
     pl.semaphore_signal(barrier, inc=1, device_id=sibling, device_id_type=MESH)
     for t in range(3):
-        for step in (1, -1):
+        for step in (1, -1, 2):
             pl.semaphore_signal(
                 barrier, inc=1, device_id=out_shares[t].along(0, step), device_id_type=MESH
             )
@@ -266,15 +285,15 @@
         return pltpu.make_async_copy(wqkv_hbm.at[rows, columns], qkv.at[to, pl.ds(0, D)], w_sem.at[slot])
 
     weight_copy(0, 0).start()
-    pl.semaphore_wait(barrier, 14)
-
-    def send(src, dst, send_sems, recv_sems, d):
+    pl.semaphore_wait(barrier, 17)
+
+    def send(src, dst, send_sems, recv_sems, d, h):
         p = (chip + d) % 8
         return pltpu.make_async_remote_copy(
-            src_ref=src.at[p],
-            dst_ref=dst.at[:, own_frame],
-            send_sem=send_sems.at[d],
-            recv_sem=recv_sems.at[d],
+            src_ref=src.at[p, pl.ds(2 * h, 2)],
+            dst_ref=dst.at[pl.ds(2 * h, 2), own_frame],
+            send_sem=send_sems.at[h, d],
+            recv_sem=recv_sems.at[h, d],
             device_id=peer(d),
             device_id_type=MESH,
         )
@@ -285,17 +304,21 @@
             device_id=device, device_id_type=MESH,
         )
 
-    def arrival(dst, send_sems, recv_sems, d):
-        return same_place(dst.at[:, frame_from(d, core)], send_sems, recv_sems, d, peer(d))
-
-    def forward(dst, send_sems, recv_sems, d):
-        return same_place(dst.at[:, frame_from(d, core)], send_sems, recv_sems, d, sibling)
-
-    def forwarded(dst, send_sems, recv_sems, d):
-        return same_place(dst.at[:, frame_from(d, 1 - core)], send_sems, recv_sems, d, sibling)
-
-    for d in range(1, 8):
-        send(x_hbm, xl, xs_sem, xr_sem, d).start()
+    def arrival(dst, send_sems, recv_sems, d, h):
+        view = dst.at[pl.ds(2 * h, 2), frame_from(d, core)]
+        return same_place(view, send_sems.at[h], recv_sems.at[h], d, peer(d))
+
+    def forward(dst, send_sems, recv_sems, d, h):
+        view = dst.at[pl.ds(2 * h, 2), frame_from(d, core)]
+        return same_place(view, send_sems.at[h], recv_sems.at[h], d, sibling)
+
+    def forwarded(dst, send_sems, recv_sems, d, h):
+        view = dst.at[pl.ds(2 * h, 2), frame_from(d, 1 - core)]
+        return same_place(view, send_sems.at[h], recv_sems.at[h], d, sibling)
+
+    for h in range(2):
+        for d in range(1, 8):
+            send(x_hbm, xl, xs_sem, xr_sem, d, h).start()
 
     load_g.wait()
     same = iota((256, 256), 0) == iota((256, 256), 1)
@@ -314,7 +337,8 @@
         sel[n] = jnp.where(hit, 1.0, 0.0).astype(BF16)
 
     load_x.wait()
-    forward(xl, xfs_sem, xfr_sem, 0).start()
+    for h in range(2):
+        forward(xl, xfs_sem, xfr_sem, 0, h).start()
 
     def head_copy(a):
         return pltpu.make_async_copy(
@@ -348,12 +372,18 @@
 
     own_g = pltpu.make_async_copy(gsrc.at[chip], gl.at[:, own_frame], loc_sem.at[2])
     own_g.start()
-    for d in range(1, 8):
-        send(x_hbm, xl, xs_sem, xr_sem, d).wait_send()
-        send(gsrc, gl, gs_sem, gr_sem, d).start()
-    for d in range(1, 8):
-        arrival(xl, xs_sem, xr_sem, d).wait_recv()
-        forward(xl, xfs_sem, xfr_sem, d).start()
+    for h in range(2):
+        for d in range(1, 8):
+            send(gsrc, gl, gs_sem, gr_sem, d, h).start()
+
+    def pass_on(dst, sems, h):
+        for d in range(1, 8):
+            arrival(dst, sems[0], sems[1], d, h).wait_recv()
+            forward(dst, sems[2], sems[3], d, h).start()
+
+    x_sems = (xs_sem, xr_sem, xfs_sem, xfr_sem)
+    g_sems = (gs_sem, gr_sem, gfs_sem, gfr_sem)
+    pass_on(xl, x_sems, 0)
 
     for a in range(LOCAL):
         head_copy(a).wait()
@@ -367,10 +397,11 @@
         gqkv[:, PART * part + 512 : PART * part + 640] = jnp.zeros((128, 128), F32)
     mixed[:, 512:640] = jnp.zeros((128, 128), F32)
 
+    own_g.wait()
+    for h in range(2):
+        forward(gl, gfs_sem, gfr_sem, 0, h).start()
     for d in range(8):
-        forwarded(xl, xfs_sem, xfr_sem, d).wait_recv()
-    own_g.wait()
-    forward(gl, gfs_sem, gfr_sem, 0).start()
+        forwarded(xl, xfs_sem, xfr_sem, d, 0).wait_recv()
 
     def split_x(g, carry):
         rows = pl.ds(pl.multiple_of(g * 128, 128), 128)
@@ -386,25 +417,33 @@
             xtl2[80 * i : 80 * i + 80, rows] = low[144 * i + 64 : 144 * i + 144]
         return carry
 
-    lax.fori_loop(0, 4, split_x, 0)
-
-    def project(first, width):
+    def project(h, first, width):
         to = pl.ds(first, width)
-        qkv[:, to] = dot3(
-            big_h[:, 0:D], big_l[:, 0:D], wph[:, to], wpl[:, to], NN
-        )
-
-    def project_tile(n, carry):
-        project(pl.multiple_of(n * 256, 256), 256)
-        return carry
-
-    lax.fori_loop(0, 7, project_tile, 0)
-    project(1792, 128)
+        rows = pl.ds(256 * h, 256)
+        qkv[rows, to] = dot3(
+            big_h[rows, 0:D], big_l[rows, 0:D], wph[:, to], wpl[:, to], NN
+        )
+
+    def project_half(h):
+        def project_tile(n, carry):
+            project(h, pl.multiple_of(n * 256, 256), 256)
+            return carry
+
+        lax.fori_loop(0, 7, project_tile, 0)
+        project(h, 1792, 128)
+
+    lax.fori_loop(0, 2, split_x, 0)
+    pass_on(xl, x_sems, 1)
+    project_half(0)
     for d in range(8):
-        forward(xl, xfs_sem, xfr_sem, d).wait_send()
-    for d in range(1, 8):
-        arrival(gl, gs_sem, gr_sem, d).wait_recv()
-        forward(gl, gfs_sem, gfr_sem, d).start()
+        forwarded(xl, xfs_sem, xfr_sem, d, 1).wait_recv()
+    lax.fori_loop(2, 4, split_x, 0)
+    project_half(1)
+    for h in range(2):
+        for d in range(8):
+            forward(xl, xfs_sem, xfr_sem, d, h).wait_send()
+    pass_on(gl, g_sems, 0)
+    pass_on(gl, g_sems, 1)
 
     scaling = HEAD_DIM ** (-0.5)
     firsts = [min(HEAD_DIM * a // 128 * 128, 384) for a in range(LOCAL)]
@@ -440,8 +479,9 @@
 
     lax.fori_loop(0, 4, attend, 0)
 
-    for d in range(8):
-        forwarded(gl, gfs_sem, gfr_sem, d).wait_recv()
+    for h in range(2):
+        for d in range(8):
+            forwarded(gl, gfs_sem, gfr_sem, d, h).wait_recv()
 
     def regroup(g, carry):
         rows = pl.ds(pl.multiple_of(g * 128, 128), 128)
@@ -571,7 +611,6 @@
     middle(out_shares, 0)
     lax.fori_loop(2, 4, attend_back, 0)
     close(out_shares, 0)
-    open_stage(out_shares, 1)
 
     def gw_copies(which, j, slot):
         copies = []
@@ -631,9 +670,6 @@
     for share in first_shares:
         for copy in share.loads():
             copy.start()
-    middle(out_shares, 1)
-    close(out_shares, 1)
-    open_stage(out_shares, 2)
     gw_part(1)
     for share in first_shares:
         for copy in share.loads():
@@ -643,8 +679,6 @@
     for share in second_shares:
         for copy in share.loads():
             copy.start()
-    middle(out_shares, 2)
-    close(out_shares, 2)
 
     def gi_cross(p):
         return pltpu.make_async_remote_copy(
@@ -672,10 +706,12 @@
     def gi_arrival(d):
         return same_place(input_out.at[(chip + 8 - d) % 8], ga_send, ga_recv, d, peer(d))
 
-    for d in range(1, 8):
-        send(gsrc, gl, gs_sem, gr_sem, d).wait_send()
-    for d in range(8):
-        forward(gl, gfs_sem, gfr_sem, d).wait_send()
+    for h in range(2):
+        for d in range(1, 8):
+            send(x_hbm, xl, xs_sem, xr_sem, d, h).wait_send()
+            send(gsrc, gl, gs_sem, gr_sem, d, h).wait_send()
+        for d in range(8):
+            forward(gl, gfs_sem, gfr_sem, d, h).wait_send()
 
     def input_tile(first, width):
         to = pl.ds(first, width)
@@ -691,7 +727,8 @@
     for p in range(8):
         gi_cross(p).start()
     close(first_shares, 0)
-    open_stage(first_shares, 1)
+    early = out_shares + first_shares
+    open_stage(early, 1)
     for share in second_shares:
         for copy in share.loads():
             copy.wait()
@@ -701,20 +738,26 @@
         gi_crossed(p).wait_recv()
         mine = 2 * p + core
         gl[:, mine] = gl[:, mine] + xl[:, mine]
-        if d:
-            gi_back(d).start()
     own_input = pltpu.make_async_copy(gl.at[:, own_frame], input_out.at[chip], fin_sem.at[0])
     own_input.start()
-    middle(first_shares, 1)
+
+    def return_input(*ds):
+        for d in ds:
+            gi_back(d).start()
+
+    return_input(1, 2)
+    middle(early, 1)
+    return_input(3)
     close(second_shares, 0)
     open_stage(second_shares, 1)
-    close(first_shares, 1)
-    open_stage(first_shares, 2)
+    close(early, 1)
+    open_stage(early, 2)
+    return_input(4)
     middle(second_shares, 1)
-    middle(first_shares, 2)
+    return_input(5, 6, 7)
     close(second_shares, 1)
     open_stage(second_shares, 2)
-    close(first_shares, 2)
+    close(early, 2)
 
     def swap(start, size, sem):
         return pltpu.make_async_remote_copy(
@@ -725,7 +768,6 @@
 
     swaps = (swap(0, TOPS[2], 1), swap(TOPS[2], SHARE - TOPS[2], 3))
     swaps[0].start()
-    middle(second_shares, 2)
     close(second_shares, 2)
     swaps[1].start()
     swaps[0].wait_recv()
@@ -813,8 +855,8 @@
         vmem((4, 2, 72, D), F32),
         vmem((SHARE, 128), F32),
         vmem((SHARE, 128), F32),
-        dma((8,)), dma((8,)), dma((8,)), dma((8,)),
-        dma((8,)), dma((8,)), dma((8,)), dma((8,)),
+        dma((2, 8)), dma((2, 8)), dma((2, 8)), dma((2, 8)),
+        dma((2, 8)), dma((2, 8)), dma((2, 8)), dma((2, 8)),
         dma((3,)), dma((10,)), dma((2, 2, 6)), dma((8, 6)),
         dma((9, 3, 6)), dma((9, 3, 6)), dma((9, 3)),
         dma((8,)), dma((8,)), dma((8,)), dma((8,)), dma((5,)),

time: 171 us -> 147 us (0.86)
  Pallas kernels: 167 us -> 142 us
    pallas_call x1, Pallas kernels: 167 us -> 142 us  [on_device(): pl.pallas_call(kernel, out_shape=[shape((8, 4, 8, D), F32), shape((144, 2...]
where the time goes in v4:
time: 147 us; the launch traced here: 146 us
  Pallas kernels  142 us (97%)
  local copies, waits for them, and re-layouts  3.7 us (3%)
    pallas_call x1, Pallas kernels, on_device(): pl.pallas_call(kernel, out_shape=[shape((8, 4, 8, D), F32), shape((144, 2...  142 us
    unnamed x7, local copies, waits for them, and re-layouts  3.7 us

profile of v4, /device:TPU:1, one launch (start us, length us, event | category | flops | bytes accessed | tf_op | source)
XLA Modules:
  0.0 146.5 jit_solution(2816279763220986355)
XLA Ops:
  0.6 142.1 %shard_map.76 = (f32[8,4,8,1152]{3,2,1,0:T(8,128)}, f32[144,216]{1,0:T(8,128)}, f32[144,72]{1,0:T(8,128)}, f32[4,4,4,24,128]{4,3,2,1,0:T(8,128)}, f32[4,4,4,24,1...) custom-call(f32[8,4,8,1152]{3,2,1,0:T(8,128)} %bitcast.5, ...), custom_call_target="tpu_custom_call" | custom-call | flops 23000000512 | bytes 60000000 | tf_op jit(solution)/shard_map/pallas_call | solution.py:870
  142.8 0.0 copy-start
  142.8 0.0 copy-start.1
  142.8 2.4 %copy.11 = f32[1,1,256,1152]{3,2,1,0:T(8,128)} copy(f32[1,1,256,1152]{3,2,1,0:T(8,128)} %bitcast.4) | data formatting | bytes 2359296
  145.2 0.0 copy-done
  145.2 0.7 copy.12
  145.8 0.0 copy-done.1
  145.8 0.6 copy.13
Async XLA Ops:
  142.8 2.4 %copy-start = (f32[144,216]{1,0:T(8,128)S(1)}, f32[144,216]{1,0:T(8,128)}, u32[]{:S(2)}) copy-start(f32[144,216]{1,0:T(8,128)} %get-tuple-element.13) | copy-start | bytes 373252
  142.8 3.1 %copy-start.1 = (f32[144,72]{1,0:T(8,128)S(1)}, f32[144,72]{1,0:T(8,128)}, u32[]{:S(2)}) copy-start(f32[144,72]{1,0:T(8,128)} %get-tuple-element.14) | copy-start | bytes 124420

commit v5 on v4

--- a/solution.py
+++ b/solution.py
@@ -11,7 +11,7 @@
 D = 1152
 LOCAL = 8
 PART = 640
-PARTS = ((24, 24, 24), (40, 40, 48), (48, 48, 64))
+PARTS = ((24, 24, 24), (32, 40, 56), (48, 40, 72))
 TOPS = (0, 72, 200)
 SHARE = 360
 CUTS = ((0, 64), (64, 80))
@@ -278,13 +278,15 @@
     load_g = pltpu.make_async_copy(g_hbm, gsrc, loc_sem.at[1])
     load_g.start()
 
-    def weight_copy(step, slot):
-        rows = pl.ds(pl.multiple_of((step % 6) * 192, 8), 192)
-        columns = pl.ds(pl.multiple_of((step // 6) * D, 128), D)
-        to = pl.ds(pl.multiple_of(slot * 192, 8), 192)
+    def weight_copy(step):
+        rows = pl.ds(pl.multiple_of((step % 9) * 128, 8), 128)
+        columns = pl.ds(pl.multiple_of((step // 9) * D, 128), D)
+        slot = step % 4
+        to = pl.ds(pl.multiple_of(slot * 128, 8), 128)
         return pltpu.make_async_copy(wqkv_hbm.at[rows, columns], qkv.at[to, pl.ds(0, D)], w_sem.at[slot])
 
-    weight_copy(0, 0).start()
+    for step in range(3):
+        weight_copy(step).start()
     pl.semaphore_wait(barrier, 17)
 
     def send(src, dst, send_sems, recv_sems, d, h):
@@ -327,6 +329,11 @@
     column = column.reshape(8, 4, 8, 1)
     for p in range(8):
         gsrc[p] = gsrc[p] * column[p]
+    own_g = pltpu.make_async_copy(gsrc.at[chip], gl.at[:, own_frame], loc_sem.at[2])
+    own_g.start()
+    for h in range(2):
+        for d in range(1, 8):
+            send(gsrc, gl, gs_sem, gr_sem, d, h).start()
 
     bases = (0, 128, 384, 640, 640)
     for n in range(5):
@@ -344,37 +351,30 @@
         return pltpu.make_async_copy(
             wout_hbm.at[pl.ds(HEAD_DIM * (2 * a + core), HEAD_DIM)],
             outw.at[a // 2, a % 2],
-            w_sem.at[2 + a],
+            w_sem.at[4 + a],
         )
 
     for a in range(LOCAL):
         head_copy(a).start()
 
     def prepare(step, carry):
-        slot = step % 2
-
-        @pl.when(step < 17)
+        @pl.when(step < 24)
         def _():
-            weight_copy(step + 1, 1 - slot).start()
-
-        weight_copy(step, slot).wait()
-        rows = pl.ds(pl.multiple_of((step % 6) * 192, 16), 192)
-        staged = pl.ds(pl.multiple_of(slot * 192, 8), 192)
-        part = step // 6
+            weight_copy(step + 3).start()
+
+        weight_copy(step).wait()
+        rows = pl.ds(pl.multiple_of((step % 9) * 128, 16), 128)
+        staged = pl.ds(pl.multiple_of((step % 4) * 128, 8), 128)
+        part = step // 9
         for n in range(5):
-            high, low = split(qkv[staged, bases[n] : bases[n] + 512])
+            both = stack(*split(qkv[staged, bases[n] : bases[n] + 512]))
+            both = dot(both, sel[n], NN).astype(BF16)
             to = pl.ds(pl.multiple_of(PART * part + 128 * n, 128), 128)
-            wph[rows, to] = dot(high, sel[n], NN).astype(BF16)
-            wpl[rows, to] = dot(low, sel[n], NN).astype(BF16)
+            wph[rows, to] = both[0:128]
+            wpl[rows, to] = both[128:256]
         return carry
 
-    lax.fori_loop(0, 18, prepare, 0)
-
-    own_g = pltpu.make_async_copy(gsrc.at[chip], gl.at[:, own_frame], loc_sem.at[2])
-    own_g.start()
-    for h in range(2):
-        for d in range(1, 8):
-            send(gsrc, gl, gs_sem, gr_sem, d, h).start()
+    lax.fori_loop(0, 27, prepare, 0)
 
     def pass_on(dst, sems, h):
         for d in range(1, 8):
@@ -857,7 +857,7 @@
         vmem((SHARE, 128), F32),
         dma((2, 8)), dma((2, 8)), dma((2, 8)), dma((2, 8)),
         dma((2, 8)), dma((2, 8)), dma((2, 8)), dma((2, 8)),
-        dma((3,)), dma((10,)), dma((2, 2, 6)), dma((8, 6)),
+        dma((3,)), dma((12,)), dma((2, 2, 6)), dma((8, 6)),
         dma((9, 3, 6)), dma((9, 3, 6)), dma((9, 3)),
         dma((8,)), dma((8,)), dma((8,)), dma((8,)), dma((5,)),
     ]

time: 147 us -> 147 us (level)
  no operation moved by 1% of the time
where the time goes in v5:
time: 147 us; the launch traced here: 146 us
  Pallas kernels  142 us (97%)
  local copies, waits for them, and re-layouts  3.7 us (3%)
    pallas_call x1, Pallas kernels, on_device(): pl.pallas_call(kernel, out_shape=[shape((8, 4, 8, D), F32), shape((144, 2...  142 us
    unnamed x7, local copies, waits for them, and re-layouts  3.7 us

profile of v5, /device:TPU:1, one launch (start us, length us, event | category | flops | bytes accessed | tf_op | source)
XLA Modules:
  0.0 146.5 jit_solution(4405946058701503938)
XLA Ops:
  0.6 142.1 %shard_map.76 = (f32[8,4,8,1152]{3,2,1,0:T(8,128)}, f32[144,216]{1,0:T(8,128)}, f32[144,72]{1,0:T(8,128)}, f32[4,4,4,24,128]{4,3,2,1,0:T(8,128)}, f32[4,4,4,24,1...) custom-call(f32[8,4,8,1152]{3,2,1,0:T(8,128)} %bitcast.5, ...), custom_call_target="tpu_custom_call" | custom-call | flops 23000000512 | bytes 60000000 | tf_op jit(solution)/shard_map/pallas_call | solution.py:870
  142.7 0.0 copy-start
  142.7 0.0 copy-start.1
  142.8 2.4 %copy.11 = f32[1,1,256,1152]{3,2,1,0:T(8,128)} copy(f32[1,1,256,1152]{3,2,1,0:T(8,128)} %bitcast.4) | data formatting | bytes 2359296
  145.2 0.0 copy-done
  145.2 0.7 copy.12
  145.8 0.0 copy-done.1
  145.8 0.6 copy.13
Async XLA Ops:
  142.7 2.4 %copy-start = (f32[144,216]{1,0:T(8,128)S(1)}, f32[144,216]{1,0:T(8,128)}, u32[]{:S(2)}) copy-start(f32[144,216]{1,0:T(8,128)} %get-tuple-element.13) | copy-start | bytes 373252
  142.7 3.1 %copy-start.1 = (f32[144,72]{1,0:T(8,128)S(1)}, f32[144,72]{1,0:T(8,128)}, u32[]{:S(2)}) copy-start(f32[144,72]{1,0:T(8,128)} %get-tuple-element.14) | copy-start | bytes 124420

commit v6 on v5

--- a/solution.py
+++ b/solution.py
@@ -82,8 +82,8 @@
         return pltpu.make_async_remote_copy(
             src_ref=self.source(stage, far, half),
             dst_ref=self.ones[stage].at[half, pl.ds(0, size)],
-            send_sem=self.send_sem.at[self.index, stage, half],
-            recv_sem=self.recv_sem.at[self.index, stage, half],
+            send_sem=self.send_sem.at[self.index, stage],
+            recv_sem=self.recv_sem.at[self.index, 3 * stage + half],
             device_id=self.along(stage, 1 if half == 0 else -1),
             device_id_type=MESH,
         )
@@ -95,12 +95,11 @@
             src = self.ones[stage].at[half, pl.ds(0, size)]
         else:
             src = self.source(stage, up if way == 0 else down, half)
-        slot = 2 + 2 * way + half
         return pltpu.make_async_remote_copy(
             src_ref=src,
             dst_ref=self.twos[stage].at[way, pl.ds(start, size)],
-            send_sem=self.send_sem.at[self.index, stage, slot],
-            recv_sem=self.recv_sem.at[self.index, stage, slot],
+            send_sem=self.send_sem.at[self.index, stage],
+            recv_sem=self.recv_sem.at[self.index, 3 * stage + 2],
             device_id=self.along(stage, 1 if way == 0 else -1),
             device_id_type=MESH,
         )
@@ -110,8 +109,8 @@
         return pltpu.make_async_remote_copy(
             src_ref=self.sources[2].at[(self.spots(2)[0] + step + 4) % 4],
             dst_ref=self.three.at[way],
-            send_sem=self.send_sem.at[self.index, 2, way],
-            recv_sem=self.recv_sem.at[self.index, 2, way],
+            send_sem=self.send_sem.at[self.index, 2],
+            recv_sem=self.recv_sem.at[self.index, 6],
             device_id=self.along(2, step),
             device_id_type=MESH,
         )
@@ -119,11 +118,15 @@
     def loads(self):
         me, up, down, far = self.spots(0)
         copy = pltpu.make_async_copy
+        sem = self.load_sem.at[self.index]
         return (
-            copy(self.source(0, up, 0), self.load.at[0], self.load_sem.at[self.index, 0]),
-            copy(self.source(0, down, 1), self.load.at[1], self.load_sem.at[self.index, 1]),
-            copy(self.gw.at[me], self.sources[1], self.load_sem.at[self.index, 2]),
-        )
+            copy(self.source(0, up, 0), self.load.at[0], sem),
+            copy(self.source(0, down, 1), self.load.at[1], sem),
+            copy(self.gw.at[me], self.sources[1], sem),
+        )
+
+    def wait_loads(self):
+        wait_copy(self.gw.at[pl.ds(0, 2)], self.load_sem.at[self.index])
 
     def middle(self, stage):
         me, up, down, far = self.spots(stage)
@@ -140,14 +143,11 @@
     def close(self, stage):
         me = self.spots(stage)[0]
         if stage == 2:
-            for way in range(3):
-                self.direct(way).wait_recv()
+            wait_copy(self.three, self.recv_sem.at[self.index, 6])
             self.last[...] = self.sources[2][me] + self.three[0] + self.three[1] + self.three[2]
             return
-        for way in range(2):
-            for half in range(2):
-                self.second_hop(stage, way, half).wait_recv()
         two = self.twos[stage]
+        wait_copy(two, self.recv_sem.at[self.index, 3 * stage + 2])
         if stage == 0:
             own = self.sources[1]
             own[...] = own[...] + two[0] + two[1]
@@ -156,13 +156,9 @@
             own[...] = self.sources[1][me] + two[0] + two[1]
 
     def finish(self):
-        for stage in range(2):
-            for half in range(2):
-                self.first_hop(stage, half).wait_send()
-                for way in range(2):
-                    self.second_hop(stage, way, half).wait_send()
-        for way in range(3):
-            self.direct(way).wait_send()
+        wait_copy(self.gw.at[pl.ds(0, 3)], self.send_sem.at[self.index, 0])
+        wait_copy(self.gw.at[0, pl.ds(0, 3)], self.send_sem.at[self.index, 1])
+        wait_copy(self.gw.at[0, 0, pl.ds(0, 3)], self.send_sem.at[self.index, 2])
 
 
 def open_stage(shares, stage):
@@ -294,29 +290,28 @@
         return pltpu.make_async_remote_copy(
             src_ref=src.at[p, pl.ds(2 * h, 2)],
             dst_ref=dst.at[pl.ds(2 * h, 2), own_frame],
-            send_sem=send_sems.at[h, d],
+            send_sem=send_sems.at[0],
             recv_sem=recv_sems.at[h, d],
             device_id=peer(d),
             device_id_type=MESH,
         )
 
-    def same_place(view, send_sems, recv_sems, d, device):
+    def same_place(view, send_sem, recv_sem, device):
         return pltpu.make_async_remote_copy(
-            src_ref=view, dst_ref=view, send_sem=send_sems.at[d], recv_sem=recv_sems.at[d],
+            src_ref=view, dst_ref=view, send_sem=send_sem, recv_sem=recv_sem,
             device_id=device, device_id_type=MESH,
         )
 
     def arrival(dst, send_sems, recv_sems, d, h):
         view = dst.at[pl.ds(2 * h, 2), frame_from(d, core)]
-        return same_place(view, send_sems.at[h], recv_sems.at[h], d, peer(d))
+        return same_place(view, send_sems.at[0], recv_sems.at[h, d], peer(d))
 
     def forward(dst, send_sems, recv_sems, d, h):
         view = dst.at[pl.ds(2 * h, 2), frame_from(d, core)]
-        return same_place(view, send_sems.at[h], recv_sems.at[h], d, sibling)
-
-    def forwarded(dst, send_sems, recv_sems, d, h):
-        view = dst.at[pl.ds(2 * h, 2), frame_from(d, 1 - core)]
-        return same_place(view, send_sems.at[h], recv_sems.at[h], d, sibling)
+        return same_place(view, send_sems.at[0], recv_sems.at[h], sibling)
+
+    def wait_forwarded(dst, recv_sems, h):
+        wait_copy(dst.at[pl.ds(2 * h, 2), pl.ds(0, 8)], recv_sems.at[h])
 
     for h in range(2):
         for d in range(1, 8):
@@ -351,7 +346,7 @@
         return pltpu.make_async_copy(
             wout_hbm.at[pl.ds(HEAD_DIM * (2 * a + core), HEAD_DIM)],
             outw.at[a // 2, a % 2],
-            w_sem.at[4 + a],
+            w_sem.at[4],
         )
 
     for a in range(LOCAL):
@@ -385,8 +380,7 @@
     g_sems = (gs_sem, gr_sem, gfs_sem, gfr_sem)
     pass_on(xl, x_sems, 0)
 
-    for a in range(LOCAL):
-        head_copy(a).wait()
+    wait_copy(outw, w_sem.at[4])
     for n in range(4):
         high, low = split(outw[n].reshape(144, D))
         woh[144 * n : 144 * n + 144, :] = high
@@ -400,8 +394,7 @@
     own_g.wait()
     for h in range(2):
         forward(gl, gfs_sem, gfr_sem, 0, h).start()
-    for d in range(8):
-        forwarded(xl, xfs_sem, xfr_sem, d, 0).wait_recv()
+    wait_forwarded(xl, xfr_sem, 0)
 
     def split_x(g, carry):
         rows = pl.ds(pl.multiple_of(g * 128, 128), 128)
@@ -435,13 +428,10 @@
     lax.fori_loop(0, 2, split_x, 0)
     pass_on(xl, x_sems, 1)
     project_half(0)
-    for d in range(8):
-        forwarded(xl, xfs_sem, xfr_sem, d, 1).wait_recv()
+    wait_forwarded(xl, xfr_sem, 1)
     lax.fori_loop(2, 4, split_x, 0)
     project_half(1)
-    for h in range(2):
-        for d in range(8):
-            forward(xl, xfs_sem, xfr_sem, d, h).wait_send()
+    wait_copy(xl.at[:, pl.ds(0, 8)], xfs_sem.at[0])
     pass_on(gl, g_sems, 0)
     pass_on(gl, g_sems, 1)
 
@@ -480,8 +470,7 @@
     lax.fori_loop(0, 4, attend, 0)
 
     for h in range(2):
-        for d in range(8):
-            forwarded(gl, gfs_sem, gfr_sem, d, h).wait_recv()
+        wait_forwarded(gl, gfr_sem, h)
 
     def regroup(g, carry):
         rows = pl.ds(pl.multiple_of(g * 128, 128), 128)
@@ -534,7 +523,7 @@
             for t, target in enumerate(targets(0, 2 * dx_high + j % 2, j // 2)):
                 copies.append(
                     pltpu.make_async_copy(
-                        outw.at[:, dx_high, pl.ds(24 * t, 24), columns], target, out_sem.at[j, 3 * dx_high + t]
+                        outw.at[:, dx_high, pl.ds(24 * t, 24), columns], target, out_sem.at[0]
                     )
                 )
         return copies
@@ -544,11 +533,6 @@
             copy.start()
         return carry
 
-    def out_wait(j, carry):
-        for copy in out_copies(j):
-            copy.wait()
-        return carry
-
     lax.fori_loop(0, 8, out_start, 0)
 
     for first, width in ((0, 256), (256, 256), (512, 128)):
@@ -556,14 +540,13 @@
             gqh[:, 0:D], gql[:, 0:D], woh[first : first + width, :], wol[first : first + width, :], NT
         )
 
-    lax.fori_loop(0, 8, out_wait, 0)
+    wait_copy(outw.at[:, :, :, pl.ds(0, 1024)], out_sem.at[0])
     open_stage(out_shares, 0)
     for share in out_shares:
         for copy in share.loads():
             copy.start()
     for share in out_shares:
-        for copy in share.loads():
-            copy.wait()
+        share.wait_loads()
 
     def attend_back(g, carry):
         rows = pl.ds(pl.multiple_of(g * 128, 128), 128)
@@ -618,11 +601,15 @@
             for t, target in enumerate(targets(1 + which, 2 * dx_high + j % 2, j // 2)):
                 copies.append(
                     pltpu.make_async_copy(
-                        stage_refs[which][t].at[slot, dx_high], target, gw_sem.at[which, slot, 3 * dx_high + t]
+                        stage_refs[which][t].at[slot, dx_high], target, gw_sem.at[which, slot, t]
                     )
                 )
         return copies
 
+    def wait_gw(which, slot):
+        for t in range(3):
+            wait_copy(stage_refs[which][t].at[slot], gw_sem.at[which, slot, t])
+
     def gw_part(which):
         high_ref, low_ref = ((xth1, xtl1), (xth2, xtl2))[which]
         size = CUTS[which][1]
@@ -632,8 +619,7 @@
 
             @pl.when(j >= 2)
             def _():
-                for copy in gw_copies(which, j - 2, slot):
-                    copy.wait()
+                wait_gw(which, slot)
 
             to = pl.ds(pl.multiple_of(j * 256, 256), 256)
             term = dot3(high_ref[...], low_ref[...], big_h[:, to], big_l[:, to], NN)
@@ -661,9 +647,8 @@
             return carry
 
         lax.fori_loop(0, 8, gw_step, 0)
-        for j in (6, 7):
-            for copy in gw_copies(which, j, j % 2):
-                copy.wait()
+        for slot in range(2):
+            wait_gw(which, slot)
 
     gw_part(0)
     open_stage(first_shares, 0)
@@ -672,8 +657,7 @@
             copy.start()
     gw_part(1)
     for share in first_shares:
-        for copy in share.loads():
-            copy.wait()
+        share.wait_loads()
     middle(first_shares, 0)
     open_stage(second_shares, 0)
     for share in second_shares:
@@ -684,34 +668,25 @@
         return pltpu.make_async_remote_copy(
             src_ref=gl.at[:, 2 * p + 1 - core],
             dst_ref=xl.at[:, 2 * p + 1 - core],
-            send_sem=gx_send.at[p],
-            recv_sem=gx_recv.at[p],
+            send_sem=gx_send.at[0],
+            recv_sem=gx_recv.at[0],
             device_id=sibling,
             device_id_type=MESH,
         )
-
-    def gi_crossed(p):
-        return same_place(xl.at[:, 2 * p + core], gx_send, gx_recv, p, sibling)
 
     def gi_back(d):
         return pltpu.make_async_remote_copy(
             src_ref=gl.at[:, 2 * ((chip + d) % 8) + core],
             dst_ref=input_out.at[chip],
-            send_sem=ga_send.at[d],
-            recv_sem=ga_recv.at[d],
+            send_sem=ga_send.at[0],
+            recv_sem=ga_recv.at[0],
             device_id=peer(d),
             device_id_type=MESH,
         )
 
-    def gi_arrival(d):
-        return same_place(input_out.at[(chip + 8 - d) % 8], ga_send, ga_recv, d, peer(d))
-
-    for h in range(2):
-        for d in range(1, 8):
-            send(x_hbm, xl, xs_sem, xr_sem, d, h).wait_send()
-            send(gsrc, gl, gs_sem, gr_sem, d, h).wait_send()
-        for d in range(8):
-            forward(gl, gfs_sem, gfr_sem, d, h).wait_send()
+    wait_copy(x_hbm.at[pl.ds(0, 7)], xs_sem.at[0])
+    wait_copy(gsrc.at[pl.ds(0, 7)], gs_sem.at[0])
+    wait_copy(gl.at[:, pl.ds(0, 8)], gfs_sem.at[0])
 
     def input_tile(first, width):
         to = pl.ds(first, width)
@@ -730,12 +705,11 @@
     early = out_shares + first_shares
     open_stage(early, 1)
     for share in second_shares:
-        for copy in share.loads():
-            copy.wait()
+        share.wait_loads()
     middle(second_shares, 0)
+    wait_copy(xl.at[:, pl.ds(0, 8)], gx_recv.at[0])
     for d in range(8):
         p = (chip + d) % 8
-        gi_crossed(p).wait_recv()
         mine = 2 * p + core
         gl[:, mine] = gl[:, mine] + xl[:, mine]
     own_input = pltpu.make_async_copy(gl.at[:, own_frame], input_out.at[chip], fin_sem.at[0])
@@ -807,11 +781,9 @@
     out_out[0:72, :] = jnp.where(even, a, b)[:, 0:HEAD_DIM]
     out_out[72:144, :] = jnp.where(even, b, a)[:, 0:HEAD_DIM]
 
-    for d in range(1, 8):
-        gi_arrival(d).wait_recv()
-        gi_back(d).wait_send()
-    for p in range(8):
-        gi_cross(p).wait_send()
+    wait_copy(input_out.at[pl.ds(0, 7)], ga_recv.at[0])
+    wait_copy(gl.at[:, pl.ds(0, 7)], ga_send.at[0])
+    wait_copy(gl.at[:, pl.ds(0, 8)], gx_send.at[0])
     for share in shares:
         share.finish()
     for copy in swaps:
@@ -855,11 +827,11 @@
         vmem((4, 2, 72, D), F32),
         vmem((SHARE, 128), F32),
         vmem((SHARE, 128), F32),
-        dma((2, 8)), dma((2, 8)), dma((2, 8)), dma((2, 8)),
-        dma((2, 8)), dma((2, 8)), dma((2, 8)), dma((2, 8)),
-        dma((3,)), dma((12,)), dma((2, 2, 6)), dma((8, 6)),
-        dma((9, 3, 6)), dma((9, 3, 6)), dma((9, 3)),
-        dma((8,)), dma((8,)), dma((8,)), dma((8,)), dma((5,)),
+        dma((1,)), dma((2, 8)), dma((1,)), dma((2,)),
+        dma((1,)), dma((2, 8)), dma((1,)), dma((2,)),
+        dma((3,)), dma((5,)), dma((2, 2, 3)), dma((1,)),
+        dma((9, 3)), dma((9, 7)), dma((9,)),
+        dma((1,)), dma((1,)), dma((1,)), dma((1,)), dma((5,)),
     ]
     for part in (1, 2):
         scratch += [vmem((2, 2, 4, rows, 128), F32) for rows in PARTS[part]]

time: 147 us -> 142 us (0.966)
  Pallas kernels: 142 us -> 138 us
    pallas_call x1, Pallas kernels: 142 us -> 138 us  [on_device(): pl.pallas_call(kernel, out_shape=[shape((8, 4, 8, D), F32), shape((144, 2...]
where the time goes in v6:
time: 142 us
  Pallas kernels  138 us (97%)
  local copies, waits for them, and re-layouts  3.7 us (3%)
    pallas_call x1, Pallas kernels, on_device(): pl.pallas_call(kernel, out_shape=[shape((8, 4, 8, D), F32), shape((144, 2...  138 us
    unnamed x7, local copies, waits for them, and re-layouts  3.7 us

profile of v6, /device:TPU:1, one launch (start us, length us, event | category | flops | bytes accessed | tf_op | source)
XLA Modules:
  0.0 142.2 jit_solution(15578492395484420392)
XLA Ops:
  0.6 137.8 %shard_map.76 = (f32[8,4,8,1152]{3,2,1,0:T(8,128)}, f32[144,216]{1,0:T(8,128)}, f32[144,72]{1,0:T(8,128)}, f32[4,4,4,24,128]{4,3,2,1,0:T(8,128)}, f32[4,4,4,24,1...) custom-call(f32[8,4,8,1152]{3,2,1,0:T(8,128)} %bitcast.5, ...), custom_call_target="tpu_custom_call" | custom-call | flops 23000000512 | bytes 60000000 | tf_op jit(solution)/shard_map/pallas_call | solution.py:842
  138.4 0.0 copy-start
  138.4 0.0 copy-start.1
  138.5 2.4 %copy.11 = f32[1,1,256,1152]{3,2,1,0:T(8,128)} copy(f32[1,1,256,1152]{3,2,1,0:T(8,128)} %bitcast.4) | data formatting | bytes 2359296
  140.9 0.0 copy-done
  140.9 0.7 copy.12
  141.5 0.0 copy-done.1
  141.5 0.6 copy.13
Async XLA Ops:
  138.4 2.4 %copy-start = (f32[144,216]{1,0:T(8,128)S(1)}, f32[144,216]{1,0:T(8,128)}, u32[]{:S(2)}) copy-start(f32[144,216]{1,0:T(8,128)} %get-tuple-element.13) | copy-start | bytes 373252
  138.4 3.1 %copy-start.1 = (f32[144,72]{1,0:T(8,128)S(1)}, f32[144,72]{1,0:T(8,128)}, u32[]{:S(2)}) copy-start(f32[144,72]{1,0:T(8,128)} %get-tuple-element.14) | copy-start | bytes 124420

commit v7 on v6

--- a/solution.py
+++ b/solution.py
@@ -330,13 +330,12 @@
         for d in range(1, 8):
             send(gsrc, gl, gs_sem, gr_sem, d, h).start()
 
-    bases = (0, 128, 384, 640, 640)
-    for n in range(5):
-        lane = iota((512, 128), 1) + 128 * n
-        head = lane // HEAD_DIM
-        source = lane + HEAD_DIM * (head + core) - bases[n]
-        hit = (iota((512, 128), 0) == source) & (lane < LOCAL * HEAD_DIM)
-        sel[n] = jnp.where(hit, 1.0, 0.0).astype(BF16)
+    tiles = ((0, 256, 0, 640), (256, 256, 384, 768), (512, 128, 640, 512))
+    for first, width, base, depth in tiles:
+        lane = iota((depth, width), 1) + first
+        source = lane + HEAD_DIM * (lane // HEAD_DIM + core) - base
+        hit = (iota((depth, width), 0) == source) & (lane < LOCAL * HEAD_DIM)
+        sel[0:depth, first : first + width] = jnp.where(hit, 1.0, 0.0).astype(BF16)
 
     load_x.wait()
     for h in range(2):
@@ -361,10 +360,10 @@
         rows = pl.ds(pl.multiple_of((step % 9) * 128, 16), 128)
         staged = pl.ds(pl.multiple_of((step % 4) * 128, 8), 128)
         part = step // 9
-        for n in range(5):
-            both = stack(*split(qkv[staged, bases[n] : bases[n] + 512]))
-            both = dot(both, sel[n], NN).astype(BF16)
-            to = pl.ds(pl.multiple_of(PART * part + 128 * n, 128), 128)
+        for first, width, base, depth in tiles:
+            both = stack(*split(qkv[staged, base : base + depth]))
+            both = dot(both, sel[0:depth, first : first + width], NN).astype(BF16)
+            to = pl.ds(pl.multiple_of(PART * part + first, 128), width)
             wph[rows, to] = both[0:128]
             wpl[rows, to] = both[128:256]
         return carry
@@ -802,7 +801,7 @@
         vmem((4, 16, 8, D), F32),
         vmem((4, 16, 8, D), F32),
         vmem((8, 4, 8, D), F32),
-        vmem((5, 512, 128), BF16),
+        vmem((768, PART), BF16),
         vmem((D, 3 * PART), BF16),
         vmem((D, 3 * PART), BF16),
         vmem((PART, D), BF16),

time: 142 us -> 143 us (level)
  no operation moved by 1% of the time
where the time goes in v7:
time: 143 us
  Pallas kernels  139 us (97%)
  local copies, waits for them, and re-layouts  3.7 us (3%)
    pallas_call x1, Pallas kernels, on_device(): pl.pallas_call(kernel, out_shape=[shape((8, 4, 8, D), F32), shape((144, 2...  139 us
    unnamed x7, local copies, waits for them, and re-layouts  3.7 us

profile of v7, /device:TPU:1, one launch (start us, length us, event | category | flops | bytes accessed | tf_op | source)
XLA Modules:
  0.0 142.9 jit_solution(6855355823432985787)
XLA Ops:
  0.6 138.5 %shard_map.76 = (f32[8,4,8,1152]{3,2,1,0:T(8,128)}, f32[144,216]{1,0:T(8,128)}, f32[144,72]{1,0:T(8,128)}, f32[4,4,4,24,128]{4,3,2,1,0:T(8,128)}, f32[4,4,4,24,1...) custom-call(f32[8,4,8,1152]{3,2,1,0:T(8,128)} %bitcast.5, ...), custom_call_target="tpu_custom_call" | custom-call | flops 23000000512 | bytes 60000000 | tf_op jit(solution)/shard_map/pallas_call | solution.py:841
  139.2 0.0 copy-start
  139.2 0.0 copy-start.1
  139.2 2.4 %copy.11 = f32[1,1,256,1152]{3,2,1,0:T(8,128)} copy(f32[1,1,256,1152]{3,2,1,0:T(8,128)} %bitcast.4) | data formatting | bytes 2359296
  141.6 0.0 copy-done
  141.6 0.7 copy.12
  142.2 0.0 copy-done.1
  142.2 0.6 copy.13
Async XLA Ops:
  139.2 2.4 %copy-start = (f32[144,216]{1,0:T(8,128)S(1)}, f32[144,216]{1,0:T(8,128)}, u32[]{:S(2)}) copy-start(f32[144,216]{1,0:T(8,128)} %get-tuple-element.13) | copy-start | bytes 373252
  139.2 3.1 %copy-start.1 = (f32[144,72]{1,0:T(8,128)S(1)}, f32[144,72]{1,0:T(8,128)}, u32[]{:S(2)}) copy-start(f32[144,72]{1,0:T(8,128)} %get-tuple-element.14) | copy-start | bytes 124420
